TPU v7x, 512 devices: a whole 4x8x8 slice. The times are simulated.
512 devices in a mesh: grp: 32 (over x, y), dev: 16 (over z, core).
Axes of the slice: x: 4, y: 8, z: 8, core: 2. Of those that a mesh axis runs over, the one named last changes fastest.
Arguments:
- design: float32 [262144, 1024], P(('grp', 'dev')), as said below
- observed: float32 [262144], P(('grp', 'dev')), may hold values from -6 to 6
- row_weight: float32 [262144], P(('grp', 'dev')), may hold values from 0.3 to 3
- arc_of_row: int32 [262144, 1], P(('grp', 'dev')), may hold values from 0 to 31, as said below
- prior_factor: float32 [1024, 1024], P('dev'), as said below
- prior_rhs: float32 [1024], P('dev'), may hold values from -6 to 6
Outputs:
- new_factor: float32 [1024, 1024], P('dev')
- new_rhs: float32 [1024], P('dev')
Inputs may be any that keep to these rules, and one draw needn't show every extreme that they name: `arc_of_row`: arc numbers count within a group of 16 devices along dev; arc a of a group is owned by the device of index a // 2 in that group. Among the rows of one device no arc stands more than 24 times. In every group the arcs of one owner stand exactly 24 times among the rows of every device of that group. `prior_factor`: upper triangular with diagonal between 1 and 2. `design`: entries below 1 in magnitude.
All inputs are finite; a program needn't handle non-finite values.
Results may differ from a plain program's by a relative error of at most 0.0013.
Values sent between devices are 32-bit elements; how exact they have to be, the bound alone decides.
No kernel may reach another device: no remote copies, remote signals or barrier semaphores. Data moves between devices by JAX's collectives and lax.ppermute only.
A program may use at most 128 MiB of HBM per device.

v0:
```python
import jax
import jax.numpy as jnp
from jax import lax
from jax.sharding import PartitionSpec as P

ARCS_DEV = 2


bias_prior = 1.0


def inner(left, right):
    return lax.dot_general(
        left,
        right,
        (((0,), (0,)), ((), ())),
        precision=lax.Precision.HIGHEST,
        preferred_element_type=jnp.float32,
    )


def on_device(design, observed, row_weight, arc_of_row, prior_factor, prior_rhs):
    n_dev = lax.axis_size("dev")
    row_count, width = design.shape
    arcs_group = ARCS_DEV * n_dev
    arc_index = arc_of_row[:, 0]
    onehot = (arc_index[:, None] == jnp.arange(arcs_group, dtype=jnp.int32)[None, :]).astype(
        jnp.float32
    )
    weighted = row_weight[:, None] * design
    scaled_obs = row_weight * observed
    most = max(row_count * 3 // (2 * arcs_group), 2)
    slots = ARCS_DEV * most
    owner_dev = arc_index // ARCS_DEV
    within_arc = arc_index % ARCS_DEV
    earlier = jnp.tril(jnp.ones((row_count, row_count), jnp.float32), -1)
    row_rank = jnp.sum(
        jnp.dot(earlier, onehot, precision=lax.Precision.HIGHEST) * onehot, axis=1
    ).astype(jnp.int32)
    target = owner_dev * slots + within_arc * most + row_rank
    buffer = (
        jnp.zeros((n_dev * slots, width), jnp.float32)
        .at[target]
        .set(weighted)
        .reshape(n_dev, slots, width)
    )
    pairs = jnp.stack([row_weight, scaled_obs], axis=1)
    side_info = (
        jnp.zeros((n_dev * slots, 2), jnp.float32).at[target].set(pairs).reshape(n_dev, slots, 2)
    )
    side_info = jnp.transpose(side_info, (0, 2, 1))
    got_rows, got_side = (
        lax.all_to_all(buffer, "dev", split_axis=0, concat_axis=0, tiled=True),
        lax.all_to_all(side_info, "dev", split_axis=0, concat_axis=0, tiled=True),
    )
    data_rows = got_rows.reshape(n_dev * slots, width)
    weights = got_side[:, 0, :].reshape(n_dev, ARCS_DEV, most)
    obs_got = got_side[:, 1, :].reshape(n_dev, ARCS_DEV, most)
    data_obs = got_side[:, 1, :].reshape(-1)
    arc_sum = jnp.einsum(
        "sam,samp->ap",
        weights,
        got_rows.reshape(n_dev, ARCS_DEV, most, width),
        precision=lax.Precision.HIGHEST,
    )
    total = jnp.sum(weights * weights, axis=(0, 2)) + bias_prior
    obs_sum = jnp.sum(weights * obs_got, axis=(0, 2))
    scaled_arcs = arc_sum / total[:, None]
    include = (lax.axis_index("grp") == 0).astype(jnp.float32)
    prior_local = prior_factor * include
    projected = (
        inner(data_rows, data_obs) + inner(prior_local, prior_rhs) - inner(arc_sum, obs_sum / total)
    )
    projected = lax.psum(projected, ("grp", "dev"))
    block = lax.psum_scatter(
        inner(data_rows, data_rows) + inner(prior_local, prior_local) - inner(scaled_arcs, arc_sum),
        "dev",
        scatter_dimension=0,
        tiled=True,
    )
    block = lax.psum(block, "grp")
    gram = lax.all_gather(block, "dev", axis=0, tiled=True)
    lower = jnp.linalg.cholesky(gram)
    solved = lax.linalg.triangular_solve(lower, projected[:, None], left_side=True, lower=True)[
        :, 0
    ]
    share = width // n_dev
    first_row = lax.axis_index("dev") * share
    factor_rows = lax.dynamic_slice_in_dim(lower, first_row, share, 1).T
    rhs_rows = lax.dynamic_slice_in_dim(solved, first_row, share, 0)
    return (factor_rows, rhs_rows)


def solution(mesh):
    placed = (
        P(("grp", "dev"), None),
        P(("grp", "dev")),
        P(("grp", "dev")),
        P(("grp", "dev"), None),
        P("dev", None),
        P("dev"),
    )
    return jax.shard_map(
        on_device, mesh=mesh, in_specs=placed, out_specs=(P("dev", None), P("dev")), check_vma=False
    )
```

profile of v0, /device:TPU:1, one launch (start us, length us, event | category | flops | bytes accessed | tf_op | source)
XLA Modules:
  0.0 801.1 jit_solution(8580317421086242565)
XLA Ops:
  13.6 11.8 %all-to-all-start.1 = ((f32[16,2,48]{2,1,0:T(2,128)}), f32[16,2,48]{2,1,0:T(2,128)S(1)}, u32[]{:S(2)}, u32[]{:S(2)}) async-start(f32[16,2,48]{2,1,0:T(2,128)} %bitcast.8), calls=%async_computation.1 | async-start | bytes 32768 | tf_op jit(solution)/shard_map/all_to_all | solution.py:54
  44.1 65.0 %all-to-all-done = f32[16,48,1024]{2,1,0:T(8,128)S(1)} async-done(((f32[16,48,1024]{2,1,0:T(8,128)}), f32[16,48,1024]{2,1,0:T(8,128)S(1)}, u32[]{:S(2)}, u32[]{:S(2)}) %all-to-all-start) | async-done | bytes 3145760 | tf_op jit(solution)/shard_map/all_to_all | solution.py:53
  110.8 11.0 %fusion.104 = f32[1024,1024,1]{1,0,2:T(8,128)S(1)} fusion(f32[16,48,1024]{2,1,0:T(8,128)S(1)} %all-to-all-done), kind=kOutput, calls=%fused_computation.228 | convolution fusion | flops 9663676416 | bytes 7340032 | tf_op jit(solution)/shard_map/dot_general | solution.py:13
  121.9 5.7 fusion.1
  127.7 62.3 %reduce-scatter.4.cloned.1.call-done = f32[64,1024]{1,0:T(8,128)} async-done(((f32[1024,1024]{1,0:T(8,128)}), f32[64,1024]{1,0:T(8,128)}) %reduce-scatter.4.cloned.1.call-update) | async-done | bytes 262160
  192.0 156.2 %all-reduce.3.cloned.1.call-done = f32[64,1024]{0,1:T(8,128)} async-done(((f32[64,1024]{0,1:T(8,128)}), f32[64,1024]{0,1:T(8,128)}) %all-reduce.3.cloned.1.call-update) | async-done | bytes 262160 | tf_op jit(solution)/shard_map/psum | solution.py:81
  352.6 101.9 %psum.15 = f32[1024]{0:T(1024)S(1)} all-reduce(f32[1024]{0:T(1024)S(1)} %add_subtract_fusion), channel_id=1, replica_groups=mesh['grp'=32,'dev'=16] {'grp','dev'}, use_global_device_ids=true, to_apply=%region_25.26 | all-reduce | flops 1024 | bytes 8192 | tf_op jit(solution)/shard_map/psum | solution.py:74
  466.2 11.7 %cholesky.223 = f32[128,128]{1,0:T(8,128)S(1)} custom-call(f32[128,128]{1,0:T(8,128)S(1)} %cholesky.580), custom_call_target="Cholesky" | custom-call | tf_op jit(solution)/shard_map/jit(cholesky)/cholesky | solution.py:83
  478.0 9.8 %custom-call.62 = f32[1,128,128]{1,2,0:T(8,128)S(1)} custom-call(f32[1,128,128]{2,1,0:T(8,128)S(1)} %get-tuple-element.55), custom_call_target="InvertDiagBlocksLowerTriangular" | custom-call | tf_op jit(solution)/shard_map/jit(cholesky)/cholesky | solution.py:83
  494.0 12.1 %cholesky.244 = f32[128,128]{1,0:T(8,128)S(1)} custom-call(f32[128,128]{1,0:T(8,128)S(1)} %cholesky.584), custom_call_target="Cholesky" | custom-call | tf_op jit(solution)/shard_map/jit(cholesky)/cholesky | solution.py:83
  507.7 9.8 %custom-call.63 = f32[1,128,128]{1,2,0:T(8,128)S(1)} custom-call(f32[1,128,128]{2,1,0:T(8,128)S(1)} %get-tuple-element.52), custom_call_target="InvertDiagBlocksLowerTriangular" | custom-call | tf_op jit(solution)/shard_map/jit(cholesky)/cholesky | solution.py:83
  520.8 11.7 %cholesky.468 = f32[128,128]{1,0:T(8,128)S(1)} custom-call(f32[128,128]{1,0:T(8,128)S(1)} %cholesky.589), custom_call_target="Cholesky" | custom-call | tf_op jit(solution)/shard_map/jit(cholesky)/cholesky | solution.py:83
  533.8 9.8 %custom-call.64 = f32[1,128,128]{1,2,0:T(8,128)S(1)} custom-call(f32[1,128,128]{2,1,0:T(8,128)S(1)} %get-tuple-element.49), custom_call_target="InvertDiagBlocksLowerTriangular" | custom-call | tf_op jit(solution)/shard_map/jit(cholesky)/cholesky | solution.py:83
  547.2 11.9 %cholesky.487 = f32[128,128]{1,0:T(8,128)S(1)} custom-call(f32[128,128]{1,0:T(8,128)S(1)} %cholesky.594), custom_call_target="Cholesky" | custom-call | tf_op jit(solution)/shard_map/jit(cholesky)/cholesky | solution.py:83
  560.4 9.8 %custom-call.65 = f32[1,128,128]{1,2,0:T(8,128)S(1)} custom-call(f32[1,128,128]{2,1,0:T(8,128)S(1)} %get-tuple-element.46), custom_call_target="InvertDiagBlocksLowerTriangular" | custom-call | tf_op jit(solution)/shard_map/jit(cholesky)/cholesky | solution.py:83
  573.7 11.7 %cholesky.506 = f32[128,128]{1,0:T(8,128)S(1)} custom-call(f32[128,128]{1,0:T(8,128)S(1)} %cholesky.599), custom_call_target="Cholesky" | custom-call | tf_op jit(solution)/shard_map/jit(cholesky)/cholesky | solution.py:83
  586.7 10.2 %custom-call.66 = f32[1,128,128]{1,2,0:T(8,128)S(1)} custom-call(f32[1,128,128]{2,1,0:T(8,128)S(1)} %get-tuple-element.43), custom_call_target="InvertDiagBlocksLowerTriangular" | custom-call | tf_op jit(solution)/shard_map/jit(cholesky)/cholesky | solution.py:83
  600.2 11.7 %cholesky.526 = f32[128,128]{1,0:T(8,128)S(1)} custom-call(f32[128,128]{1,0:T(8,128)S(1)} %cholesky.604), custom_call_target="Cholesky" | custom-call | tf_op jit(solution)/shard_map/jit(cholesky)/cholesky | solution.py:83
  613.3 9.8 %custom-call.67 = f32[1,128,128]{1,2,0:T(8,128)S(1)} custom-call(f32[1,128,128]{2,1,0:T(8,128)S(1)} %get-tuple-element.40), custom_call_target="InvertDiagBlocksLowerTriangular" | custom-call | tf_op jit(solution)/shard_map/jit(cholesky)/cholesky | solution.py:83
  626.0 11.8 %cholesky.546 = f32[128,128]{1,0:T(8,128)S(1)} custom-call(f32[128,128]{1,0:T(8,128)S(1)} %cholesky.609), custom_call_target="Cholesky" | custom-call | tf_op jit(solution)/shard_map/jit(cholesky)/cholesky | solution.py:83
  639.2 9.8 %custom-call.68 = f32[1,128,128]{1,2,0:T(8,128)S(1)} custom-call(f32[1,128,128]{2,1,0:T(8,128)S(1)} %get-tuple-element.37), custom_call_target="InvertDiagBlocksLowerTriangular" | custom-call | tf_op jit(solution)/shard_map/jit(cholesky)/cholesky | solution.py:83
  651.6 11.7 %cholesky.564 = f32[128,128]{1,0:T(8,128)S(1)} custom-call(f32[128,128]{1,0:T(8,128)S(1)} %convolution_subtract_fusion.6), custom_call_target="Cholesky" | custom-call | tf_op jit(solution)/shard_map/jit(cholesky)/cholesky | solution.py:83
  676.2 27.6 %while.1 = (s32[]{:T(128)}, f32[1024,1024]{1,0:T(8,128)}, s32[8,2]{0,1:T(2,128)S(1)}, f32[8,128,128]{2,1,0:T(8,128)}, s32[]{:T(128)}) while((s32[]{:T(128)}, f32[1024,1024]{1,0:T(8,128)}, s32[8,2]{0,1:T(2,128)S(1)}, f32[8,128,128]{2,1,0:T(8,128)}, s32[]{:T(128)}) %tuple.68), condition=%wide.while_cond, body=%wide.while_body.sunk | while | flops 2 | bytes 132205 | solution.py:84
  703.9 79.4 %custom-call.69 = f32[8,128,128]{1,2,0:T(8,128)S(1)} custom-call(f32[8,128,128]{2,1,0:T(8,128)} %get-tuple-element.9), custom_call_target="InvertDiagBlocksLowerTriangular" | custom-call | tf_op jit(solution)/shard_map/triangular_solve | solution.py:84
  (130 shorter events, 125.1 us)
Async XLA Ops:
  7.2 343.0 %copy-start = (f32[64]{0:T(128)S(1)}, f32[64]{0:T(128)}, u32[]{:S(2)}) copy-start(f32[64]{0:T(128)} %param.11) | copy-start | bytes 772
  13.6 19.2 %all-to-all-start.1 = ((f32[16,2,48]{2,1,0:T(2,128)}), f32[16,2,48]{2,1,0:T(2,128)S(1)}, u32[]{:S(2)}, u32[]{:S(2)}) async-start(f32[16,2,48]{2,1,0:T(2,128)} %bitcast.8), calls=%async_computation.1 | async-start | bytes 32768 | tf_op jit(solution)/shard_map/all_to_all | solution.py:54
  30.8 7.4 copy-start.3
  32.8 76.3 %all-to-all-start = ((f32[16,48,1024]{2,1,0:T(8,128)}), f32[16,48,1024]{2,1,0:T(8,128)S(1)}, u32[]{:S(2)}, u32[]{:S(2)}) async-start(f32[16,48,1024]{2,1,0:T(8,128)} %bitcast.231), calls=%async_computation | async-start | bytes 6291456 | tf_op jit(solution)/shard_map/all_to_all | solution.py:53
  38.1 151.8 %reduce-scatter.4.cloned.1.call-start = ((), (), s32[]{:S(2)}) async-start(), calls=%async_computation.5 | async-start | bytes 4456448
  110.8 11.1 %copy-start.1 = (f32[1024,1024]{1,0:T(8,128)S(1)}, f32[1024,1024]{1,0:T(8,128)}, u32[]{:S(2)}) copy-start(f32[1024,1024]{1,0:T(8,128)} %fusion.49) | copy-start | bytes 12582916
  127.6 220.5 %all-reduce.3.cloned.1.call-start = ((), (), s32[]{:S(2)}) async-start(), calls=%async_computation.3 | async-start | bytes 1048576 | tf_op jit(solution)/shard_map/psum | solution.py:81
  191.9 262.5 %all-gather.2.cloned.1.call-start = ((), (), s32[]{:S(2)}) async-start(), calls=%async_computation.4 | async-start | bytes 4456448 | tf_op jit(solution)/shard_map/all_gather | solution.py:82
  464.3 1.9 copy-start.2
Sparse Core Ops, SparseCore 0:
  127.8 62.1 reduce-scatter.3
  193.4 154.7 all-reduce.2
  351.1 47.5 all-gather.1
where the time goes:
time: 808 us; the launch traced here: 801 us
  waiting for transfers between devices  286 us (35%)
  other arithmetic  269 us (33%)
  blocking collectives  102 us (13%)
  matrix products  61 us (8%)
  local copies, waits for them, and re-layouts  47.1 us (6%)
  between operations  19.3 us (2%)
  starting transfers between devices  17.3 us (2%)
    another operation x30, other arithmetic, on_device(): lower = jnp.linalg.cholesky(gram)  173 us
    psum x1, waiting for transfers between devices, on_device(): block = lax.psum(block, 'grp')  156 us
    psum x1, blocking collectives, on_device(): projected = lax.psum(projected, ('grp', 'dev'))  102 us
    another operation x3, other arithmetic, on_device(): lax.linalg.triangular_solve(lower, projected[:, None], left_side=True, lo...  84.2 us
    all_to_all x1, waiting for transfers between devices, on_device(): lax.all_to_all(buffer, 'dev', split_axis=0, concat_axis=0, tiled=True)  65 us
    unnamed x4, waiting for transfers between devices  62.3 us
    another operation x24, local copies, waits for them, and re-layouts  27.6 us
    dot_general x6, matrix products, inner(): lax.dot_general(left, right, (((0,), (0,)), ((), ())), precision=lax.Prec...  24.4 us
  transfers between devices with their start and end apart: 5, of which 4 were waited for; matrix products, arithmetic and copies ran while one was open for 2% of the time, Pallas kernels for 0%

commit v1 on v0

v1 whole, which is shorter than its diff:
```python
import functools

import jax
import jax.numpy as jnp
from jax import lax
from jax.experimental import pallas as pl
from jax.experimental.pallas import tpu as pltpu
from jax.sharding import Mesh
from jax.sharding import PartitionSpec as P

f32 = jnp.float32
bf16 = jnp.bfloat16
NB = 128
bias_prior = 1.0
VMEM = pl.BlockSpec(memory_space=pltpu.VMEM)
SMEM = pl.BlockSpec(memory_space=pltpu.SMEM)


def spread(x, i):
    return jnp.broadcast_to(x[i:i+1, :], (8, x.shape[1]))

def across(x, lane):
    return jnp.broadcast_to(x[:, lane:lane+1], (8, 128))

def split(x):
    hi = x.astype(bf16)
    rest = x - hi.astype(f32)
    mid = rest.astype(bf16)
    return hi, mid, (rest - mid.astype(f32)).astype(bf16)

def left_stack(x, axis):
    h, m, l = split(x)
    return jnp.concatenate([h, h, m, m, h, l], axis=axis)

def right_stack(x, axis):
    h, m, l = split(x)
    return jnp.concatenate([h, m, h, m, l, h], axis=axis)

def dot(a, b, ca, cb):
    return lax.dot_general(a, b, (((ca,), (cb,)), ((), ())), preferred_element_type=f32)

def factor_block(rows):
    sub = lax.broadcasted_iota(jnp.int32, (8, 128), 0)
    lane = lax.broadcasted_iota(jnp.int32, (8, 128), 1)
    n = 16
    left = list(rows)
    right = [jnp.where(lane == sub + 8 * b, 1.0, 0.0).astype(f32) for b in range(n)]
    up, inv = [], []
    for b in range(n):
        near = [c for c in (b, b + 1, b + 2) if c < n]
        col = [[across(left[c], 8 * b + j) for c in near] for j in range(8)]
        x, y = left[b], right[b]
        diag = jnp.zeros((8, 128), f32)
        mults = []
        for j in range(8):
            piv = spread(col[j][0], j)
            if j < 7:
                head = spread(col[j + 1][0], j)
                pre = col[j][0] * head
            q = 1.0 / piv
            diag = jnp.where(sub == j, piv, diag)
            if j < 7:
                col[j + 1][0] = col[j + 1][0] - pre * q
                factor = head * q
                for t in range(1, len(near)):
                    col[j + 1][t] = col[j + 1][t] - col[j][t] * factor
                for k in range(j + 2, 8):
                    factor = spread(col[k][0], j) * q
                    for t in range(len(near)):
                        col[k][t] = col[k][t] - col[j][t] * factor
                m = jnp.where(sub > j, col[j][0] * q, 0.0)
                x = x - m * spread(x, j)
                y = y - m * spread(y, j)
            mults.append([col[j][t] * q for t in range(1, len(near))])
        for t in range(1, len(near)):
            c = near[t]
            dx = [mults[j][t - 1] * spread(x, j) for j in range(8)]
            dy = [mults[j][t - 1] * spread(y, j) for j in range(8)]
            while len(dx) > 1:
                dx = [dx[i] + dx[i + 1] for i in range(0, len(dx), 2)]
                dy = [dy[i] + dy[i + 1] for i in range(0, len(dy), 2)]
            left[c] = left[c] - dx[0]
            right[c] = right[c] - dy[0]
        r = lax.rsqrt(diag)
        x = x * r
        y = y * r
        up.append(x); inv.append(y)
        if b + 3 < n:
            z = jnp.concatenate([x, y], axis=1)
            h = z.astype(bf16).astype(f32)
            m = (z - h).astype(bf16).astype(f32)
            l = z - h - m
            lhs = jnp.concatenate([p[:, :128] for p in (h, h, m, m, h, l)], axis=0).astype(bf16)
            rhs = jnp.concatenate([h, m, h, m, l, h], axis=0).astype(bf16)
            upd = dot(lhs, rhs, 0, 0)
            for c in range(b + 3, n):
                left[c] = left[c] - upd[8 * c:8 * c + 8, :128]
                right[c] = right[c] - upd[8 * c:8 * c + 8, 128:]
    return up, inv

def chol_body(a_ref, out_ref, nblk, width):
    for k in range(nblk):
        r0 = k * NB
        rows = [a_ref[r0 + 8*b: r0 + 8*b + 8, r0:r0 + NB] for b in range(16)]
        up, inv = factor_block(rows)
        li = lax.broadcasted_iota(jnp.int32, (NB, NB), 1)
        si = lax.broadcasted_iota(jnp.int32, (NB, NB), 0)
        out_ref[r0:r0 + NB, r0:r0 + NB] = jnp.where(li >= si, jnp.concatenate(up, axis=0), 0.0)
        t = left_stack(jnp.concatenate(inv, axis=0), 1)
        if r0 > 0:
            out_ref[r0:r0 + NB, 0:r0] = jnp.zeros((NB, r0), f32)
        pieces = []
        lo = r0 + NB
        while lo < width:
            hi = min(lo + 2 * NB - lo % (2 * NB), width)
            p = dot(t, right_stack(a_ref[r0:r0 + NB, lo:hi], 0), 1, 0)
            out_ref[r0:r0 + NB, lo:hi] = p
            pieces.append((lo, hi, p))
            lo = hi
        if k + 1 < nblk:
            full = jnp.concatenate([left_stack(p.T, 1) for lo, hi, p in pieces if lo < nblk * NB], axis=0)
            for lo, hi, p in pieces:
                top, end = r0 + NB, min(hi, nblk * NB)
                a_ref[top:end, lo:hi] = a_ref[top:end, lo:hi] - dot(full[:end - top], right_stack(p, 0), 1, 0)


def exact(a, b):
    return lax.dot_general(
        a, b, (((1,), (0,)), ((), ())), precision=lax.Precision.HIGHEST, preferred_element_type=f32
    )


def blocks_of(nblk):
    return [(i, j) for i in range(nblk) for j in range(i, nblk)]


def arcs_kernel(design_ref, weight_ref, obs_ref, arc_ref, out_ref):
    rows, width = design_ref.shape
    arcs = out_ref.shape[0]
    w = weight_ref[...]
    number = lax.broadcasted_iota(jnp.int32, (arcs, rows), 0)
    member = jnp.where(number == arc_ref[...], w * w, 0.0)
    out_ref[:, :width] = exact(member, design_ref[...])
    total = jnp.sum(member, axis=1, keepdims=True)
    obs = jnp.sum(member * obs_ref[...], axis=1, keepdims=True)
    lane = lax.broadcasted_iota(jnp.int32, (arcs, NB), 1)
    out_ref[:, width:] = jnp.where(lane == 0, obs, jnp.where(lane == 1, total, 0.0))


def gram_kernel(
    where_ref, design_ref, weight_ref, obs_ref, prior_ref, prhs_ref, keep_ref, send_ref, rows_ref, both_ref
):
    rows, width = design_ref.shape
    prows = prior_ref.shape[0]
    nblk = width // NB
    core = where_ref[0]
    include = where_ref[1].astype(f32)
    w = weight_ref[...]
    for r in range(0, rows, NB):
        column = jnp.broadcast_to(w[:, r:r + NB], (NB, NB)).T
        for c in range(0, width, NB):
            rows_ref[r:r + NB, c:c + NB] = design_ref[r:r + NB, c:c + NB] * column
    rows_ref[rows:rows + prows, :] = prior_ref[...] * include
    deep = rows + prows
    wobs = jnp.concatenate([w * obs_ref[...], prhs_ref[...]], axis=1)
    p = exact(jnp.broadcast_to(wobs, (8, deep)), rows_ref[...])
    order = blocks_of(nblk)
    half = len(order) // 2
    tall = []
    for i in range(nblk):
        z = rows_ref[:, i * NB:(i + 1) * NB]
        turned = jnp.concatenate([z[r:min(r + NB, deep)].T for r in range(0, deep, NB)], axis=1)
        h = turned.astype(bf16)
        m = (turned - h.astype(f32)).astype(bf16)
        tall.append(jnp.concatenate([h, h, m], axis=1))
    tall = jnp.concatenate(tall, axis=0)
    step = 2 * NB
    for lo in range(0, width, step):
        z = rows_ref[:, lo:lo + step]
        h = z.astype(bf16)
        m = (z - h.astype(f32)).astype(bf16)
        flat = jnp.concatenate([h, m, h], axis=0)
        g = dot(tall[:lo + step], flat, 1, 0)
        for i in range((lo + step) // NB):
            for j in (lo // NB, lo // NB + 1):
                if j >= i:
                    t = order.index((i, j))
                    both_ref[t // half, (t % half) * NB:(t % half + 1) * NB, :] = g[
                        i * NB:(i + 1) * NB, (j * NB - lo):(j * NB - lo) + NB
                    ]
    for r in range(2 * nblk):
        t = order.index((r // nblk, r // nblk))
        row = t * NB + NB - 8 + r % nblk
        both_ref[row // (half * NB), row % (half * NB):row % (half * NB) + 1, 0:64] = p[0:1, r * 64:(r + 1) * 64]
    keep_ref[...] = both_ref[core]
    send_ref[...] = both_ref[1 - core]


def pair_kernel(where_ref, mine_ref, got_ref, arcs_ref, out_ref):
    width = arcs_ref.shape[1] - NB
    nblk = width // NB
    order = blocks_of(nblk)
    half = len(order) // 2
    core = where_ref[0]
    s = arcs_ref[0:8, :]
    for r in range(8, arcs_ref.shape[0], 8):
        s = s + arcs_ref[r:r + 8, :]
    s = s + pltpu.roll(s, 4, 0)
    total = s[:, width + 1:width + 2] + bias_prior
    sub = lax.broadcasted_iota(jnp.int32, s.shape, 0)
    b = jnp.where(sub < 4, s * lax.rsqrt(jnp.broadcast_to(total, s.shape)), 0.0)
    obs = b[:, width:width + 1]
    p = jnp.sum(b[:, :width] * obs, axis=0, keepdims=True)
    h = b.astype(bf16).astype(f32)
    m = (b - h).astype(bf16).astype(f32)
    l = b - h - m
    lhs = jnp.concatenate([h, h, m, m, h, l], axis=0).astype(bf16)
    rhs = jnp.concatenate([h, m, h, m, l, h], axis=0).astype(bf16)

    def one(side):
        for t in range(half):
            i, j = order[side * half + t]
            part = dot(lhs[:, i * NB:(i + 1) * NB], rhs[:, j * NB:(j + 1) * NB], 0, 0)
            if i == j and i < 2:
                mine_row = [
                    jnp.concatenate([p[:, r * 64:(r + 1) * 64], part[NB - 8 + r % nblk:NB - 8 + r % nblk + 1, 64:]], axis=1)
                    for r in range(i * nblk, (i + 1) * nblk)
                ]
                part = jnp.concatenate([part[:NB - 8]] + mine_row, axis=0)
            out_ref[t * NB:(t + 1) * NB, :] = mine_ref[t * NB:(t + 1) * NB, :] + got_ref[t * NB:(t + 1) * NB, :] - part

    pl.when(core == 0)(functools.partial(one, 0))
    pl.when(core == 1)(functools.partial(one, 1))


def factor_kernel(where_ref, mine_ref, other_ref, out_ref, rhs_ref, a_ref, u_ref):
    n = u_ref.shape[0]
    nblk = n // NB
    order = blocks_of(nblk)
    half = len(order) // 2
    core = where_ref[0]
    first = core == 0
    for t, (i, j) in enumerate(order):
        rows = pl.ds((t % half) * NB, NB)
        a, b = (mine_ref, other_ref) if t < half else (other_ref, mine_ref)
        a_ref[i * NB:(i + 1) * NB, j * NB:(j + 1) * NB] = jnp.where(first, a[rows, :], b[rows, :])
    lane = lax.broadcasted_iota(jnp.int32, (NB, NB), 1)
    for k in range(nblk):
        d = (2 * k // nblk) * NB
        r = d + NB - 8 + (2 * k) % nblk
        line = jnp.concatenate([a_ref[r:r + 1, d:d + 64], a_ref[r + 1:r + 2, d:d + 64]], axis=1)
        a_ref[k * NB:(k + 1) * NB, n:] = jnp.where(lane == 0, jnp.broadcast_to(line, (NB, NB)).T, 0.0)
    chol_body(a_ref, u_ref, nblk, n + NB)
    share = out_ref.shape[0]
    mine = pl.ds(pl.multiple_of(where_ref[1] * share, share), share)
    out_ref[...] = u_ref[mine, :n]
    rhs_ref[...] = u_ref[mine, n:].T[0:1, :]


def call(kernel, name, where, args, outs, scratch, grant):
    return pl.pallas_call(
        kernel,
        out_shape=outs,
        in_specs=([SMEM] if where is not None else []) + [VMEM] * len(args),
        out_specs=jax.tree.map(lambda _: VMEM, outs),
        scratch_shapes=scratch,
        compiler_params=pltpu.CompilerParams(vmem_limit_bytes=grant * 2**20),
        name=name,
    )(*(() if where is None else (where,)), *args)


def like(*shape):
    return jax.ShapeDtypeStruct(shape, f32)


def on_device(design, observed, row_weight, arc_of_row, prior_factor, prior_rhs):
    rows, width = design.shape
    prows = prior_factor.shape[0]
    nx, ny, nz, nc = (lax.axis_size(a) for a in ("x", "y", "z", "core"))
    core, z = lax.axis_index("core"), lax.axis_index("z")
    arcs = 2 * nz * nc
    nblk = width // NB
    half = len(blocks_of(nblk)) // 2 * NB
    include = ((lax.axis_index("x") == 0) & (lax.axis_index("y") == 0)).astype(jnp.int32)
    weight = row_weight.reshape(1, rows)
    obs = observed.reshape(1, rows)
    arc = arc_of_row.reshape(1, rows)
    partial = call(arcs_kernel, "arcs", None, (design, weight, obs, arc), like(arcs, width + NB), [], 32)
    spread_arcs = jnp.repeat(partial.reshape(nz, 2 * nc, width + NB), nc, axis=0)
    owned = lax.all_to_all(spread_arcs, ("z", "core"), 0, 0, tiled=True)
    keep, send = call(
        gram_kernel,
        "gram",
        jnp.stack([core, include]).astype(jnp.int32),
        (design, weight, obs, prior_factor, (prior_rhs * include.astype(f32)).reshape(1, prows)),
        (like(half, NB), like(half, NB)),
        [pltpu.VMEM((rows + prows, width), f32), pltpu.VMEM((2, half, NB), f32)],
        48,
    )
    swap = [(i, 1 - i) for i in range(nc)]
    got = lax.ppermute(send, "core", swap)
    where = jnp.stack([core, z * nc + core]).astype(jnp.int32)
    v = call(
        pair_kernel, "pair", where, (keep, got, owned.reshape(-1, width + NB)), like(half, NB), [], 32
    )
    v = lax.all_to_all(v.reshape(nx, half // nx, NB), "x", 0, 0, tiled=True).sum(0)
    v = lax.all_to_all(v.reshape(ny, half // nx // ny, NB), "y", 0, 0, tiled=True).sum(0)
    v = lax.all_to_all(jnp.broadcast_to(v, (nz, *v.shape)), "z", 0, 0, tiled=True).sum(0)
    v = lax.all_to_all(jnp.broadcast_to(v, (ny, *v.shape)), "y", 0, 0, tiled=True)
    v = v.reshape(half // nx, NB)
    v = lax.all_to_all(jnp.broadcast_to(v, (nx, *v.shape)), "x", 0, 0, tiled=True)
    v = v.reshape(half, NB)
    other = lax.ppermute(v, "core", swap)
    factor, rhs = call(
        factor_kernel,
        "factor",
        where,
        (v, other),
        (like(prows, width), like(1, prows)),
        [pltpu.VMEM((width, width + NB), f32), pltpu.VMEM((width, width + NB), f32)],
        48,
    )
    return factor, rhs.reshape(prows)


def solution(mesh):
    fine = Mesh(mesh.devices.reshape(4, 8, 8, 2), ("x", "y", "z", "core"))
    every = ("x", "y", "z", "core")
    placed = (
        P(every, None),
        P(every),
        P(every),
        P(every, None),
        P(("z", "core"), None),
        P(("z", "core")),
    )
    return jax.shard_map(
        on_device,
        mesh=fine,
        in_specs=placed,
        out_specs=(P(("z", "core"), None), P(("z", "core"))),
        check_vma=False,
    )
```

time: 808 us -> 163 us (0.20)
  waiting for transfers between devices: 286 us -> 14.6 us
  other arithmetic: 269 us -> 0.93 us
  matrix products: 61 us -> 0 us
  local copies, waits for them, and re-layouts: 47.1 us -> 4.96 us
  Pallas kernels: 0 us -> 42 us
  blocking collectives: 102 us -> 78.3 us
  between operations: 19.3 us -> 0.73 us
    another operation x34 -> x2, other arithmetic: 258 us -> 0.15 us  [the longest x1 0.08 us: on_device(): jnp.stack([core, include]).astype(jnp.int32)]
    psum x1 -> x0, waiting for transfers between devices: 156 us -> none  [on_device(): block = lax.psum(block, 'grp')]
    psum x1 -> x0, blocking collectives: 102 us -> none  [on_device(): projected = lax.psum(projected, ('grp', 'dev'))]
    all_to_all x0 -> x5, blocking collectives: none -> 78.3 us  [the longest x1 20.6 us: on_device(): lax.all_to_all(v.reshape(nx, half // nx, NB), 'x', 0, 0, tiled=True).sum(0)]
    unnamed x4 -> x0, waiting for transfers between devices: 62.3 us -> none
    all_to_all x2 -> x1, waiting for transfers between devices: 67.1 us -> 12.3 us  [on_device(): owned = lax.all_to_all(spread_arcs, ('z', 'core'), 0, 0, tiled=True)]
    pallas_call x0 -> x4, Pallas kernels: none -> 42 us  [call(): pl.pallas_call(kernel, out_shape=outs, in_specs=([SMEM] if where is not N...]
    another operation x29 -> x0, matrix products: 33.2 us -> none  [the longest x14 22.8 us: on_device(): lower = jnp.linalg.cholesky(gram)]
  transfers between devices with their start and end apart: 5 -> 3, of which waited for: 4 -> 2; matrix products, arithmetic and copies ran while one was open for 2% -> 1% of each run, Pallas kernels for 0% -> 1%
where the time goes in v1:
time: 163 us
  blocking collectives  78.3 us (48%)
  Pallas kernels  42 us (26%)
  starting transfers between devices  21.3 us (13%)
  waiting for transfers between devices  14.6 us (9%)
  local copies, waits for them, and re-layouts  4.96 us (3%)
    pallas_call x4, Pallas kernels, call(): pl.pallas_call(kernel, out_shape=outs, in_specs=([SMEM] if where is not N...  42 us
    all_to_all x1, blocking collectives, on_device(): lax.all_to_all(v.reshape(nx, half // nx, NB), 'x', 0, 0, tiled=True).sum(0)  20.6 us
    all_to_all x1, blocking collectives, on_device(): lax.all_to_all(v.reshape(ny, half // nx // ny, NB), 'y', 0, 0, tiled=True)  17.6 us
    all_to_all x1, blocking collectives, on_device(): lax.all_to_all(jnp.broadcast_to(v, (nx, *v.shape)), 'x', 0, 0, tiled=True)  14.5 us
    all_to_all x1, blocking collectives, on_device(): lax.all_to_all(jnp.broadcast_to(v, (ny, *v.shape)), 'y', 0, 0, tiled=True)  13.5 us
    all_to_all x1, waiting for transfers between devices, on_device(): owned = lax.all_to_all(spread_arcs, ('z', 'core'), 0, 0, tiled=True)  12.3 us
    all_to_all x1, blocking collectives, on_device(): lax.all_to_all(jnp.broadcast_to(v, (nz, *v.shape)), 'z', 0, 0, tiled=True)  12.1 us
    ppermute x1, starting transfers between devices, on_device(): got = lax.ppermute(send, 'core', swap)  8.77 us
  transfers between devices with their start and end apart: 3, of which 2 were waited for; matrix products, arithmetic and copies ran while one was open for 1% of the time, Pallas kernels for 1%

profile of v1, /device:TPU:1, one launch (start us, length us, event | category | flops | bytes accessed | tf_op | source)
XLA Modules:
  0.0 162.8 jit_solution(18168601427636107464)
XLA Ops:
  0.6 0.1 pad_add_fusion.1.where_ref
  0.7 0.7 multiply_bitcast_fusion.prhs_ref
  1.4 1.6 copy-done
  3.0 0.9 copy-done.1
  3.9 0.7 copy-done.2
  4.6 0.7 copy-done.3
  5.3 5.6 %gram.1 = (f32[2304,128]{1,0:T(8,128)S(1)}, f32[2304,128]{1,0:T(8,128)}) custom-call(s32[2]{0:T(128)S(1)} %pad_add_fusion.1.where_ref, f32[512,1024]{1,0:T(8,128)S(1)} %copy-done, f32[1,512]{1,0:T(1,128)S(1)} %bitcast.17, f32[1,512]{1,0:T(1,128)S(1)} %bitcast.19, f32[64,1024]{1,0:T(8,128)S(1)} %copy-done.1, f32[1,64]{1,0:T(1,128)S(1)} %multiply_bitcast_fusion.prhs_ref), custom_call_target="tpu_custom_call" | custom-call | tf_op jit(solution)/shard_map/gram/pallas_call | solution.py:261
  10.9 8.8 %collective-permute-start = (f32[2304,128]{1,0:T(8,128)}, f32[2304,128]{1,0:T(8,128)S(1)}, u32[]{:S(2)}, u32[]{:S(2)}) collective-permute-start(f32[2304,128]{1,0:T(8,128)} %get-tuple-element.7), channel_id=1, source_target_pairs={{0,1},{1,0},{2,3},{3,2},{4,5},{5,4},{6,7},{7,6},{8,9},{9,8},{10,11... | collective-permute-start | bytes 3538952 | tf_op jit(solution)/shard_map/ppermute | solution.py:301
  19.7 1.2 arcs.1
  21.0 0.8 broadcast_in_dim.12
  21.7 5.1 %all-to-all-start = ((f32[16,4,1152]{2,1,0:T(4,128)}), f32[16,4,1152]{2,1,0:T(4,128)S(1)}, u32[]{:S(2)}, u32[]{:S(2)}) async-start(f32[16,4,1152]{2,1,0:T(4,128)} %bitcast.7), calls=%async_computation | async-start | bytes 589824 | tf_op jit(solution)/shard_map/all_to_all | solution.py:290
  26.9 12.3 %all-to-all-done = f32[16,4,1152]{2,1,0:T(4,128)S(1)} async-done(((f32[16,4,1152]{2,1,0:T(4,128)}), f32[16,4,1152]{2,1,0:T(4,128)S(1)}, u32[]{:S(2)}, u32[]{:S(2)}) %all-to-all-start) | async-done | bytes 294944 | tf_op jit(solution)/shard_map/all_to_all | solution.py:290
  39.2 0.1 reshape.46.arcs_ref
  39.3 1.0 pair.1
  40.3 20.6 %all_to_all.30 = f32[4,576,128]{2,1,0:T(8,128)S(1)} all-to-all(f32[4,576,128]{2,1,0:T(8,128)S(1)} %bitcast.16), channel_id=1, replica_groups=mesh['x'=4,'y'=8,'z'=8,'core'=2] {'x'}, dimensions={0} | all-to-all | bytes 2359296 | tf_op jit(solution)/shard_map/all_to_all | solution.py:306
  61.0 0.1 reduce_sum.27
  61.0 17.6 %all_to_all.31 = f32[8,72,128]{2,1,0:T(8,128)S(1)} all-to-all(f32[8,72,128]{2,1,0:T(8,128)S(1)} %bitcast.22), channel_id=1, replica_groups=mesh['x'=4,'y'=8,'z'=8,'core'=2] {'y'}, dimensions={0} | all-to-all | bytes 589824 | tf_op jit(solution)/shard_map/all_to_all | solution.py:307
  78.6 12.1 %all_to_all.32 = f32[8,72,128]{2,1,0:T(8,128)S(1)} all-to-all(f32[8,72,128]{2,1,0:T(8,128)S(1)} %broadcast_in_dim.13), channel_id=1, replica_groups=mesh['x'=4,'y'=8,'z'=8,'core'=2] {'z'}, dimensions={0} | all-to-all | bytes 589824 | tf_op jit(solution)/shard_map/all_to_all | solution.py:308
  90.8 13.5 %all_to_all.33 = f32[8,72,128]{2,1,0:T(8,128)S(1)} all-to-all(f32[8,72,128]{2,1,0:T(8,128)S(1)} %broadcast_in_dim.14), channel_id=1, replica_groups=mesh['x'=4,'y'=8,'z'=8,'core'=2] {'y'}, dimensions={0} | all-to-all | bytes 589824 | tf_op jit(solution)/shard_map/all_to_all | solution.py:309
  104.4 0.1 broadcast_in_dim.15
  104.5 14.5 %all_to_all.34 = f32[4,576,128]{2,1,0:T(8,128)S(1)} all-to-all(f32[4,576,128]{2,1,0:T(8,128)S(1)} %broadcast_in_dim.15), channel_id=1, replica_groups=mesh['x'=4,'y'=8,'z'=8,'core'=2] {'x'}, dimensions={0} | all-to-all | bytes 2359296 | tf_op jit(solution)/shard_map/all_to_all | solution.py:311
  118.9 7.5 %collective-permute-start.1 = (f32[2304,128]{1,0:T(8,128)S(1)}, f32[2304,128]{1,0:T(8,128)S(1)}, u32[]{:S(2)}, u32[]{:S(2)}) collective-permute-start(f32[2304,128]{1,0:T(8,128)S(1)} %bitcast.14), channel_id=1, source_target_pairs={{0,1},{1,0},{2,3},{3,2},{4,5},{5,4},{6,7},{7,6},{8,9},{9,8},{10,11... | collective-permute-start | bytes 3538952 | tf_op jit(solution)/shard_map/ppermute | solution.py:313
  126.4 2.3 %collective-permute-done.1.other_ref = f32[2304,128]{1,0:T(8,128)S(1)} collective-permute-done((f32[2304,128]{1,0:T(8,128)S(1)}, f32[2304,128]{1,0:T(8,128)S(1)}, u32[]{:S(2)}, u32[]{:S(2)}) %collective-permute-start.1) | collective-permute-done | bytes 1179680 | tf_op jit(solution)/shard_map/ppermute | solution.py:313
  128.7 34.1 %factor.1 = (f32[64,1024]{1,0:T(8,128)}, f32[1,64]{1,0:T(1,128)}) custom-call(s32[2]{0:T(128)S(1)} %pad_add_fusion.where_ref, f32[2304,128]{1,0:T(8,128)S(1)} %bitcast.15, f32[2304,128]{1,0:T(8,128)S(1)} %collective-permute-done.1.other_ref), custom_call_target="tpu_custom_call" | custom-call | tf_op jit(solution)/shard_map/factor/pallas_call | solution.py:261
  (13 shorter events, 0.2 us)
Async XLA Ops:
  1.4 1.6 copy-start
  3.0 0.9 copy-start.1
  3.9 0.7 copy-start.2
  4.6 0.7 copy-start.3
  5.3 14.4 %copy-start.4 = (s32[512,1]{0,1:T(1,128)S(1)}, s32[512,1]{0,1:T(1,128)}, u32[]{:S(2)}) copy-start(s32[512,1]{0,1:T(1,128)} %param.9) | copy-start | bytes 6148
  10.9 28.4 %collective-permute-start = (f32[2304,128]{1,0:T(8,128)}, f32[2304,128]{1,0:T(8,128)S(1)}, u32[]{:S(2)}, u32[]{:S(2)}) collective-permute-start(f32[2304,128]{1,0:T(8,128)} %get-tuple-element.7), channel_id=1, source_target_pairs={{0,1},{1,0},{2,3},{3,2},{4,5},{5,4},{6,7},{7,6},{8,9},{9,8},{10,11... | collective-permute-start | bytes 3538952 | tf_op jit(solution)/shard_map/ppermute | solution.py:301
  21.7 17.4 %all-to-all-start = ((f32[16,4,1152]{2,1,0:T(4,128)}), f32[16,4,1152]{2,1,0:T(4,128)S(1)}, u32[]{:S(2)}, u32[]{:S(2)}) async-start(f32[16,4,1152]{2,1,0:T(4,128)} %bitcast.7), calls=%async_computation | async-start | bytes 589824 | tf_op jit(solution)/shard_map/all_to_all | solution.py:290
  118.9 9.8 %collective-permute-start.1 = (f32[2304,128]{1,0:T(8,128)S(1)}, f32[2304,128]{1,0:T(8,128)S(1)}, u32[]{:S(2)}, u32[]{:S(2)}) collective-permute-start(f32[2304,128]{1,0:T(8,128)S(1)} %bitcast.14), channel_id=1, source_target_pairs={{0,1},{1,0},{2,3},{3,2},{4,5},{5,4},{6,7},{7,6},{8,9},{9,8},{10,11... | collective-permute-start | bytes 3538952 | tf_op jit(solution)/shard_map/ppermute | solution.py:313

commit v2 on v1

--- a/solution.py
+++ b/solution.py
@@ -13,6 +13,7 @@
 NB = 128
 bias_prior = 1.0
 VMEM = pl.BlockSpec(memory_space=pltpu.VMEM)
+FAR = pl.BlockSpec(memory_space=pltpu.HBM)
 SMEM = pl.BlockSpec(memory_space=pltpu.SMEM)
 
 
@@ -39,63 +40,62 @@
 def dot(a, b, ca, cb):
     return lax.dot_general(a, b, (((ca,), (cb,)), ((), ())), preferred_element_type=f32)
 
-def factor_block(rows):
+def factor_block(rows, tall=2, ahead=2):
     sub = lax.broadcasted_iota(jnp.int32, (8, 128), 0)
     lane = lax.broadcasted_iota(jnp.int32, (8, 128), 1)
     n = 16
     left = list(rows)
-    right = [jnp.where(lane == sub + 8 * b, 1.0, 0.0).astype(f32) for b in range(n)]
     up, inv = [], []
-    for b in range(n):
-        near = [c for c in (b, b + 1, b + 2) if c < n]
-        col = [[across(left[c], 8 * b + j) for c in near] for j in range(8)]
-        x, y = left[b], right[b]
-        diag = jnp.zeros((8, 128), f32)
+    for b in range(0, n, tall):
+        own = list(range(b, b + tall))
+        near = list(range(b + tall, min(b + tall + ahead, n)))
+        steps = 8 * tall
+        col = [{c: across(left[c], 8 * b + j) for c in own[j // 8:] + near} for j in range(steps)]
+        x = {c: left[c] for c in own}
+        y = {c: jnp.where(lane == sub + 8 * c, 1.0, 0.0) for c in own}
+        diag = {c: jnp.ones((8, 128), f32) for c in own}
         mults = []
-        for j in range(8):
-            piv = spread(col[j][0], j)
-            if j < 7:
-                head = spread(col[j + 1][0], j)
-                pre = col[j][0] * head
-            q = 1.0 / piv
-            diag = jnp.where(sub == j, piv, diag)
-            if j < 7:
-                col[j + 1][0] = col[j + 1][0] - pre * q
-                factor = head * q
-                for t in range(1, len(near)):
-                    col[j + 1][t] = col[j + 1][t] - col[j][t] * factor
-                for k in range(j + 2, 8):
-                    factor = spread(col[k][0], j) * q
-                    for t in range(len(near)):
-                        col[k][t] = col[k][t] - col[j][t] * factor
-                m = jnp.where(sub > j, col[j][0] * q, 0.0)
-                x = x - m * spread(x, j)
-                y = y - m * spread(y, j)
-            mults.append([col[j][t] * q for t in range(1, len(near))])
-        for t in range(1, len(near)):
-            c = near[t]
-            dx = [mults[j][t - 1] * spread(x, j) for j in range(8)]
-            dy = [mults[j][t - 1] * spread(y, j) for j in range(8)]
+        for j in range(steps):
+            home = own[j // 8]
+            q = 1.0 / spread(col[j][home], j % 8)
+            diag[home] = jnp.where(sub == j % 8, q, diag[home])
+            scaled = {c: col[j][c] * q for c in col[j]}
+            for k in range(j + 1, steps):
+                kh = own[k // 8]
+                head = spread(col[j][kh], k % 8)
+                for c in col[k]:
+                    col[k][c] = col[k][c] - scaled[c] * head
+            sx, sy = spread(x[home], j % 8), spread(y[home], j % 8)
+            for c in own[j // 8:]:
+                m = jnp.where(sub > j % 8, scaled[c], 0.0) if c == home else scaled[c]
+                x[c] = x[c] - m * sx
+                y[c] = y[c] - m * sy
+            mults.append(scaled)
+        done = (lane >= 8 * b) & (lane < 8 * (b + tall))
+        z = {c: jnp.where(done, y[c], x[c]) for c in own}
+        if near:
+            lines = [spread(z[own[j // 8]], j % 8) for j in range(steps)]
+        for c in near:
+            dx = [mults[j][c] * lines[j] for j in range(steps)]
             while len(dx) > 1:
                 dx = [dx[i] + dx[i + 1] for i in range(0, len(dx), 2)]
-                dy = [dy[i] + dy[i + 1] for i in range(0, len(dy), 2)]
-            left[c] = left[c] - dx[0]
-            right[c] = right[c] - dy[0]
-        r = lax.rsqrt(diag)
-        x = x * r
-        y = y * r
-        up.append(x); inv.append(y)
-        if b + 3 < n:
-            z = jnp.concatenate([x, y], axis=1)
-            h = z.astype(bf16).astype(f32)
-            m = (z - h).astype(bf16).astype(f32)
-            l = z - h - m
-            lhs = jnp.concatenate([p[:, :128] for p in (h, h, m, m, h, l)], axis=0).astype(bf16)
+            left[c] = jnp.where(done, 0.0, left[c]) - dx[0]
+        for c in own:
+            r = jnp.sqrt(diag[c])
+            up.append(x[c] * r)
+            z[c] = z[c] * r
+            inv.append(jnp.where(lane < 8 * (b + tall), z[c], 0.0))
+        after = b + tall + ahead
+        if after < n:
+            w = jnp.concatenate([z[c] for c in own], axis=0)
+            h = w.astype(bf16).astype(f32)
+            m = (w - h).astype(bf16).astype(f32)
+            l = w - h - m
+            lhs = jnp.concatenate([h, h, m, m, h, l], axis=0).astype(bf16)
             rhs = jnp.concatenate([h, m, h, m, l, h], axis=0).astype(bf16)
             upd = dot(lhs, rhs, 0, 0)
-            for c in range(b + 3, n):
-                left[c] = left[c] - upd[8 * c:8 * c + 8, :128]
-                right[c] = right[c] - upd[8 * c:8 * c + 8, 128:]
+            for c in range(after, n):
+                left[c] = jnp.where(done, 0.0, left[c]) - upd[8 * c:8 * c + 8, :]
     return up, inv
 
 def chol_body(a_ref, out_ref, nblk, width):
@@ -134,66 +134,106 @@
     return [(i, j) for i in range(nblk) for j in range(i, nblk)]
 
 
-def arcs_kernel(design_ref, weight_ref, obs_ref, arc_ref, out_ref):
+def fetch(pairs, sem):
+    copies = [pltpu.make_async_copy(src, dst, sem.at[i]) for i, (src, dst) in enumerate(pairs)]
+    for copy in copies:
+        copy.start()
+    return copies
+
+
+def row_parts(rows):
+    return [pl.ds(r, NB) for r in range(0, rows, NB)]
+
+
+def arcs_kernel(design_hbm, weight_hbm, obs_hbm, arc_hbm, out_ref, design_ref, weight_ref, obs_ref, arc_ref, sem):
     rows, width = design_ref.shape
     arcs = out_ref.shape[0]
+    parts = row_parts(rows)
+    copies = fetch(
+        [(weight_hbm, weight_ref), (arc_hbm, arc_ref), (obs_hbm, obs_ref)]
+        + [(design_hbm.at[p], design_ref.at[p]) for p in parts],
+        sem,
+    )
+    for copy in copies[:3]:
+        copy.wait()
     w = weight_ref[...]
-    number = lax.broadcasted_iota(jnp.int32, (arcs, rows), 0)
-    member = jnp.where(number == arc_ref[...], w * w, 0.0)
-    out_ref[:, :width] = exact(member, design_ref[...])
+    row = lax.broadcasted_iota(jnp.int32, (arcs, rows), 0)
+    member = jnp.where((row // 8) * 4 + row % 4 == arc_ref[...], w * w, 0.0)
     total = jnp.sum(member, axis=1, keepdims=True)
     obs = jnp.sum(member * obs_ref[...], axis=1, keepdims=True)
     lane = lax.broadcasted_iota(jnp.int32, (arcs, NB), 1)
     out_ref[:, width:] = jnp.where(lane == 0, obs, jnp.where(lane == 1, total, 0.0))
-
-
-def gram_kernel(
-    where_ref, design_ref, weight_ref, obs_ref, prior_ref, prhs_ref, keep_ref, send_ref, rows_ref, both_ref
+    sums = None
+    for n, p in enumerate(parts):
+        copies[3 + n].wait()
+        more = exact(member[:, n * NB:(n + 1) * NB], design_ref[p, :])
+        sums = more if sums is None else sums + more
+    out_ref[:, :width] = sums
+
+
+def half_kernel(mine, where_ref, tall_ref, flat_ref, p_ref, out_ref):
+    width = flat_ref.shape[1]
+    deep = flat_ref.shape[0] // 2
+    nblk = width // NB
+    order = blocks_of(nblk)
+    half = len(order) // 2
+    core = where_ref[0]
+
+    def one(side):
+        wanted = order[side * half:(side + 1) * half]
+        for lo in range(0, nblk, 2):
+            tops = sorted({i for i, j in wanted if j in (lo, lo + 1)})
+            if not tops:
+                continue
+            cols = sorted({j for i, j in wanted if j in (lo, lo + 1)})
+            c0, c1 = cols[0] * NB, cols[-1] * NB + NB
+            r0, r1 = tops[0] * NB, tops[-1] * NB + NB
+            g = dot(tall_ref[r0:r1, :], flat_ref[:, c0:c1], 1, 0)
+            g = g + dot(tall_ref[r0:r1, :deep], flat_ref[deep:, c0:c1], 1, 0)
+            for j in cols:
+                for i in tops:
+                    if (i, j) in wanted:
+                        block = g[i * NB - r0:i * NB - r0 + NB, j * NB - c0:j * NB - c0 + NB]
+                        at = wanted.index((i, j)) * NB
+                        if i == j and i < 2:
+                            corner = [p_ref[0:1, r * 64:(r + 1) * 64] for r in range(i * nblk, (i + 1) * nblk)]
+                            corner = jnp.concatenate(corner, axis=0)
+                            last = jnp.concatenate([corner, block[NB - 8:, 64:]], axis=1)
+                            block = jnp.concatenate([block[:NB - 8], last], axis=0)
+                        out_ref[at:at + NB, :] = block
+
+    pl.when(core == (0 if mine else 1))(functools.partial(one, 0))
+    pl.when(core == (1 if mine else 0))(functools.partial(one, 1))
+
+
+def first_kernel(
+    where_ref, design_ref, weight_ref, obs_ref, prior_ref, prhs_ref, after_ref, out_ref, tall_ref, flat_ref, p_ref
 ):
     rows, width = design_ref.shape
     prows = prior_ref.shape[0]
-    nblk = width // NB
-    core = where_ref[0]
+    deep = tall_ref.shape[1] // 2
     include = where_ref[1].astype(f32)
     w = weight_ref[...]
+    wobs = jnp.broadcast_to(w * w * obs_ref[...], (8, rows))
+
+    def place(r, z):
+        for c in range(0, width, NB):
+            h = z[:, c:c + NB].astype(bf16)
+            m = (z[:, c:c + NB] - h.astype(f32)).astype(bf16)
+            flat_ref[r:r + NB, c:c + NB] = m
+            flat_ref[deep + r:deep + r + NB, c:c + NB] = h
+            turned = z[:, c:c + NB].T
+            h = turned.astype(bf16)
+            tall_ref[c:c + NB, r:r + NB] = h
+            tall_ref[c:c + NB, deep + r:deep + r + NB] = (turned - h.astype(f32)).astype(bf16)
+
     for r in range(0, rows, NB):
         column = jnp.broadcast_to(w[:, r:r + NB], (NB, NB)).T
-        for c in range(0, width, NB):
-            rows_ref[r:r + NB, c:c + NB] = design_ref[r:r + NB, c:c + NB] * column
-    rows_ref[rows:rows + prows, :] = prior_ref[...] * include
-    deep = rows + prows
-    wobs = jnp.concatenate([w * obs_ref[...], prhs_ref[...]], axis=1)
-    p = exact(jnp.broadcast_to(wobs, (8, deep)), rows_ref[...])
-    order = blocks_of(nblk)
-    half = len(order) // 2
-    tall = []
-    for i in range(nblk):
-        z = rows_ref[:, i * NB:(i + 1) * NB]
-        turned = jnp.concatenate([z[r:min(r + NB, deep)].T for r in range(0, deep, NB)], axis=1)
-        h = turned.astype(bf16)
-        m = (turned - h.astype(f32)).astype(bf16)
-        tall.append(jnp.concatenate([h, h, m], axis=1))
-    tall = jnp.concatenate(tall, axis=0)
-    step = 2 * NB
-    for lo in range(0, width, step):
-        z = rows_ref[:, lo:lo + step]
-        h = z.astype(bf16)
-        m = (z - h.astype(f32)).astype(bf16)
-        flat = jnp.concatenate([h, m, h], axis=0)
-        g = dot(tall[:lo + step], flat, 1, 0)
-        for i in range((lo + step) // NB):
-            for j in (lo // NB, lo // NB + 1):
-                if j >= i:
-                    t = order.index((i, j))
-                    both_ref[t // half, (t % half) * NB:(t % half + 1) * NB, :] = g[
-                        i * NB:(i + 1) * NB, (j * NB - lo):(j * NB - lo) + NB
-                    ]
-    for r in range(2 * nblk):
-        t = order.index((r // nblk, r // nblk))
-        row = t * NB + NB - 8 + r % nblk
-        both_ref[row // (half * NB), row % (half * NB):row % (half * NB) + 1, 0:64] = p[0:1, r * 64:(r + 1) * 64]
-    keep_ref[...] = both_ref[core]
-    send_ref[...] = both_ref[1 - core]
+        place(r, design_ref[r:r + NB, :] * jnp.concatenate([column] * (width // NB), axis=1))
+    prior = prior_ref[...] * include
+    place(rows, jnp.concatenate([prior, jnp.zeros((NB - prows, width), f32)], axis=0))
+    p_ref[...] = exact(wobs, design_ref[...]) + exact(jnp.broadcast_to(prhs_ref[...], (8, prows)), prior)
+    half_kernel(False, where_ref, tall_ref, flat_ref, p_ref, out_ref)
 
 
 def pair_kernel(where_ref, mine_ref, got_ref, arcs_ref, out_ref):
@@ -257,14 +297,15 @@
     rhs_ref[...] = u_ref[mine, n:].T[0:1, :]
 
 
-def call(kernel, name, where, args, outs, scratch, grant):
+def call(kernel, name, where, args, outs, scratch, grant, far=False, cost=None):
     return pl.pallas_call(
         kernel,
         out_shape=outs,
-        in_specs=([SMEM] if where is not None else []) + [VMEM] * len(args),
+        in_specs=([SMEM] if where is not None else []) + [FAR if far else VMEM] * len(args),
         out_specs=jax.tree.map(lambda _: VMEM, outs),
         scratch_shapes=scratch,
         compiler_params=pltpu.CompilerParams(vmem_limit_bytes=grant * 2**20),
+        cost_estimate=cost,
         name=name,
     )(*(() if where is None else (where,)), *args)
 
@@ -285,17 +326,44 @@
     weight = row_weight.reshape(1, rows)
     obs = observed.reshape(1, rows)
     arc = arc_of_row.reshape(1, rows)
-    partial = call(arcs_kernel, "arcs", None, (design, weight, obs, arc), like(arcs, width + NB), [], 32)
-    spread_arcs = jnp.repeat(partial.reshape(nz, 2 * nc, width + NB), nc, axis=0)
-    owned = lax.all_to_all(spread_arcs, ("z", "core"), 0, 0, tiled=True)
-    keep, send = call(
-        gram_kernel,
-        "gram",
-        jnp.stack([core, include]).astype(jnp.int32),
-        (design, weight, obs, prior_factor, (prior_rhs * include.astype(f32)).reshape(1, prows)),
-        (like(half, NB), like(half, NB)),
-        [pltpu.VMEM((rows + prows, width), f32), pltpu.VMEM((2, half, NB), f32)],
-        48,
+    nparts = rows // NB
+    deep = rows + NB
+    here = jnp.stack([core, include]).astype(jnp.int32)
+    partial = call(
+        arcs_kernel,
+        "arcs",
+        None,
+        (design, weight, obs, arc),
+        like(2 * arcs, width + NB),
+        [
+            pltpu.VMEM((rows, width), f32),
+            pltpu.VMEM((1, rows), f32),
+            pltpu.VMEM((1, rows), f32),
+            pltpu.VMEM((1, rows), jnp.int32),
+            pltpu.SemaphoreType.DMA((3 + nparts,)),
+        ],
+        56,
+        far=True,
+    )
+    owned = lax.all_to_all(partial.reshape(nz * nc, 2 * nc, width + NB), ("z", "core"), 0, 0, tiled=True)
+    work = pl.CostEstimate(flops=2 * 10**11, bytes_accessed=10**7, transcendentals=0)
+    send, tall, flat, p = call(
+        first_kernel,
+        "first",
+        here,
+        (design, weight, obs, prior_factor, prior_rhs.reshape(1, prows), partial),
+        (
+            like(half, NB),
+            pltpu.VMEM((width, 2 * deep), bf16),
+            pltpu.VMEM((2 * deep, width), bf16),
+            pltpu.VMEM((8, width), f32),
+        ),
+        [],
+        20,
+        cost=work,
+    )
+    keep = call(
+        functools.partial(half_kernel, True), "keep", here, (tall, flat, p), pltpu.VMEM((half, NB), f32), [], 20, cost=work
     )
     swap = [(i, 1 - i) for i in range(nc)]
     got = lax.ppermute(send, "core", swap)
@@ -304,9 +372,9 @@
         pair_kernel, "pair", where, (keep, got, owned.reshape(-1, width + NB)), like(half, NB), [], 32
     )
     v = lax.all_to_all(v.reshape(nx, half // nx, NB), "x", 0, 0, tiled=True).sum(0)
-    v = lax.all_to_all(v.reshape(ny, half // nx // ny, NB), "y", 0, 0, tiled=True).sum(0)
-    v = lax.all_to_all(jnp.broadcast_to(v, (nz, *v.shape)), "z", 0, 0, tiled=True).sum(0)
-    v = lax.all_to_all(jnp.broadcast_to(v, (ny, *v.shape)), "y", 0, 0, tiled=True)
+    plane = ny * nz
+    v = lax.all_to_all(v.reshape(plane, 1, v.size // plane), ("y", "z"), 0, 0, tiled=True).sum(0)
+    v = lax.all_to_all(jnp.broadcast_to(v, (plane, *v.shape)), ("y", "z"), 0, 0, tiled=True)
     v = v.reshape(half // nx, NB)
     v = lax.all_to_all(jnp.broadcast_to(v, (nx, *v.shape)), "x", 0, 0, tiled=True)
     v = v.reshape(half, NB)
@@ -318,7 +386,7 @@
         (v, other),
         (like(prows, width), like(1, prows)),
         [pltpu.VMEM((width, width + NB), f32), pltpu.VMEM((width, width + NB), f32)],
-        48,
+        32,
     )
     return factor, rhs.reshape(prows)
 

time: 163 us -> 147 us (0.902)
  waiting for transfers between devices: 14.6 us -> 5.32 us
  Pallas kernels: 42 us -> 39 us
  local copies, waits for them, and re-layouts: 4.96 us -> 3.14 us
    all_to_all x1, waiting for transfers between devices: 12.3 us -> 3.04 us  [on_device(): lax.all_to_all(partial.reshape(nz * nc, 2 * nc, width + NB), ('z', 'core'...]
    all_to_all x1, starting transfers between devices: 5.07 us -> 11.8 us  [on_device(): lax.all_to_all(partial.reshape(nz * nc, 2 * nc, width + NB), ('z', 'core'...]
    ppermute x1, starting transfers between devices: 8.77 us -> 2.2 us  [on_device(): got = lax.ppermute(send, 'core', swap)]
    unnamed x10 -> x12, local copies, waits for them, and re-layouts: 3.91 us -> 0.03 us
    pallas_call x4 -> x5, Pallas kernels: 42 us -> 39 us  [call(): pl.pallas_call(kernel, out_shape=outs, in_specs=([SMEM] if where is not N...]
    all_to_all x3 -> x2, blocking collectives: 43.2 us -> 41 us  [the longest x1 21.9 us: on_device(): lax.all_to_all(v.reshape(plane, 1, v.size // plane), ('y', 'z'), 0, 0, ti...]
    reshape x1, local copies, waits for them, and re-layouts: 0.05 us -> 1.81 us  [on_device(): partial.reshape(nz * nc, 2 * nc, width + NB)]
  transfers between devices with their start and end apart: 3 -> 3, of which waited for: 2 -> 2; matrix products, arithmetic and copies ran while one was open for 1% -> 1% of each run, Pallas kernels for 1% -> 5%
where the time goes in v2:
time: 147 us; the launch traced here: 146 us
  blocking collectives  76.7 us (52%)
  Pallas kernels  39 us (27%)
  starting transfers between devices  20.8 us (14%)
  waiting for transfers between devices  5.32 us (4%)
  local copies, waits for them, and re-layouts  3.14 us (2%)
    pallas_call x5, Pallas kernels, call(): pl.pallas_call(kernel, out_shape=outs, in_specs=([SMEM] if where is not N...  39 us
    all_to_all x1, blocking collectives, on_device(): lax.all_to_all(v.reshape(plane, 1, v.size // plane), ('y', 'z'), 0, 0, ti...  21.9 us
    all_to_all x1, blocking collectives, on_device(): lax.all_to_all(v.reshape(nx, half // nx, NB), 'x', 0, 0, tiled=True).sum(0)  20.6 us
    all_to_all x1, blocking collectives, on_device(): lax.all_to_all(jnp.broadcast_to(v, (plane, *v.shape)), ('y', 'z'), 0, 0,...  19.1 us
    all_to_all x1, blocking collectives, on_device(): lax.all_to_all(jnp.broadcast_to(v, (nx, *v.shape)), 'x', 0, 0, tiled=True)  15.2 us
    all_to_all x1, starting transfers between devices, on_device(): lax.all_to_all(partial.reshape(nz * nc, 2 * nc, width + NB), ('z', 'core'...  11.8 us
    ppermute x1, starting transfers between devices, on_device(): other = lax.ppermute(v, 'core', swap)  6.81 us
    all_to_all x1, waiting for transfers between devices, on_device(): lax.all_to_all(partial.reshape(nz * nc, 2 * nc, width + NB), ('z', 'core'...  3.04 us
  transfers between devices with their start and end apart: 3, of which 2 were waited for; matrix products, arithmetic and copies ran while one was open for 1% of the time, Pallas kernels for 5%

profile of v2, /device:TPU:1, one launch (start us, length us, event | category | flops | bytes accessed | tf_op | source)
XLA Modules:
  0.0 146.2 jit_solution(3391614499983350334)
XLA Ops:
  0.6 3.3 %arcs.1.after_ref = f32[64,1152]{1,0:T(8,128)} custom-call(f32[512,1024]{1,0:T(8,128)} %design_ref.1, f32[1,512]{1,0:T(1,128)} %bitcast.15, f32[1,512]{1,0:T(1,128)} %bitcast.17, s32[1,512]{1,0:T(1,128)} %bitcast.22), custom_call_target="tpu_custom_call" | custom-call | tf_op jit(solution)/shard_map/arcs/pallas_call | solution.py:301
  3.9 0.0 copy-start.2
  4.0 0.0 copy-start.5
  4.0 1.8 %reshape.44 = f32[16,4,1152]{2,1,0:T(4,128)} reshape(f32[64,1152]{1,0:T(8,128)} %arcs.1.after_ref) | data formatting | bytes 589824 | tf_op jit(solution)/shard_map/reshape | solution.py:348
  5.8 11.8 %all-to-all-start = ((f32[16,4,1152]{2,1,0:T(4,128)}), f32[16,4,1152]{2,1,0:T(4,128)}, u32[]{:S(2)}, u32[]{:S(2)}) async-start(f32[16,4,1152]{2,1,0:T(4,128)} %reshape.44), calls=%async_computation | async-start | bytes 589824 | tf_op jit(solution)/shard_map/all_to_all | solution.py:348
  17.6 0.1 pad_add_fusion.1.where_ref
  17.7 4.8 %first.1 = (f32[2304,128]{1,0:T(8,128)}, bf16[1024,1280]{1,0:T(8,128)(2,1)S(1)}, bf16[1280,1024]{1,0:T(8,128)(2,1)S(1)}, f32[8,1024]{1,0:T(8,128)S(1)}) custom-call(s32[2]{0:T(128)S(1)} %pad_add_fusion.1.where_ref, f32[512,1024]{1,0:T(8,128)S(1)} %copy-done, f32[1,512]{1,0:T(1,128)S(1)} %bitcast.16, f32[1,512]{1,0:T(1,128)S(1)} %bitcast.18, ...), custom_call_target="tpu_custom_call" | custom-call | flops 199999995904 | bytes 10000000 | tf_op jit(solution)/shard_map/first/pallas_call | solution.py:301
  22.5 2.2 %collective-permute-start = (f32[2304,128]{1,0:T(8,128)}, f32[2304,128]{1,0:T(8,128)}, u32[]{:S(2)}, u32[]{:S(2)}) collective-permute-start(f32[2304,128]{1,0:T(8,128)} %get-tuple-element.11), channel_id=1, source_target_pairs={{0,1},{1,0},{2,3},{3,2},{4,5},{5,4},{6,7},{7,6},{8,9},{9,8},{10,11... | collective-permute-start | bytes 3538952 | tf_op jit(solution)/shard_map/ppermute | solution.py:369
  24.7 2.2 %keep.1.mine_ref = f32[2304,128]{1,0:T(8,128)S(1)} custom-call(s32[2]{0:T(128)S(1)} %pad_add_fusion.1.where_ref, bf16[1024,1280]{1,0:T(8,128)(2,1)S(1)} %get-tuple-element.8.tall_ref, bf16[1280,1024]{1,0:T(8,128)(2,1)S(1)} %get-tuple-element.9.flat_ref, f32[8,1024]{1,0:T(8,128)S(1)} %get-tuple-element.10.p_ref), custom_call_target="tpu_custom_call" | custom-call | flops 199999995904 | bytes 10000000 | tf_op jit(solution)/shard_map/keep/pallas_call | solution.py:301
  27.0 0.1 pad_add_fusion.where_ref
  27.1 3.0 %all-to-all-done = f32[16,4,1152]{2,1,0:T(4,128)} async-done(((f32[16,4,1152]{2,1,0:T(4,128)}), f32[16,4,1152]{2,1,0:T(4,128)}, u32[]{:S(2)}, u32[]{:S(2)}) %all-to-all-start) | async-done | bytes 294944 | tf_op jit(solution)/shard_map/all_to_all | solution.py:348
  30.1 1.1 reshape.45.arcs_ref
  31.2 1.8 %pair.1 = f32[2304,128]{1,0:T(8,128)S(1)} custom-call(s32[2]{0:T(128)S(1)} %pad_add_fusion.where_ref, f32[2304,128]{1,0:T(8,128)S(1)} %keep.1.mine_ref, f32[2304,128]{1,0:T(8,128)} %collective-permute-done.got_ref, f32[64,1152]{1,0:T(8,128)S(1)} %reshape.45.arcs_ref), custom_call_target="tpu_custom_call" | custom-call | tf_op jit(solution)/shard_map/pair/pallas_call | solution.py:301
  33.0 20.6 %all_to_all.25 = f32[4,576,128]{2,1,0:T(8,128)S(1)} all-to-all(f32[4,576,128]{2,1,0:T(8,128)S(1)} %bitcast.14), channel_id=1, replica_groups=mesh['x'=4,'y'=8,'z'=8,'core'=2] {'x'}, dimensions={0} | all-to-all | bytes 2359296 | tf_op jit(solution)/shard_map/all_to_all | solution.py:374
  53.6 0.1 reduce_sum.18
  53.7 21.9 %all_to_all.26 = f32[64,1,1152]{2,1,0:T(1,128)S(1)} all-to-all(f32[64,1,1152]{2,1,0:T(1,128)S(1)} %bitcast.20), channel_id=1, replica_groups=mesh['x'=4,'y'=8,'z'=8,'core'=2] {'y','z'}, dimensions={0} | all-to-all | bytes 589824 | tf_op jit(solution)/shard_map/all_to_all | solution.py:376
  75.5 0.2 reduce_sum.19
  75.7 0.2 broadcast_in_dim.6
  75.9 19.1 %all_to_all.27 = f32[64,1,1152]{2,1,0:T(1,128)S(1)} all-to-all(f32[64,1,1152]{2,1,0:T(1,128)S(1)} %broadcast_in_dim.6), channel_id=1, replica_groups=mesh['x'=4,'y'=8,'z'=8,'core'=2] {'y','z'}, dimensions={0} | all-to-all | bytes 589824 | tf_op jit(solution)/shard_map/all_to_all | solution.py:377
  95.0 0.1 broadcast_in_dim.7
  95.1 15.2 %all_to_all.28 = f32[4,576,128]{2,1,0:T(8,128)S(1)} all-to-all(f32[4,576,128]{2,1,0:T(8,128)S(1)} %broadcast_in_dim.7), channel_id=1, replica_groups=mesh['x'=4,'y'=8,'z'=8,'core'=2] {'x'}, dimensions={0} | all-to-all | bytes 2359296 | tf_op jit(solution)/shard_map/all_to_all | solution.py:379
  110.2 6.8 %collective-permute-start.1 = (f32[2304,128]{1,0:T(8,128)S(1)}, f32[2304,128]{1,0:T(8,128)S(1)}, u32[]{:S(2)}, u32[]{:S(2)}) collective-permute-start(f32[2304,128]{1,0:T(8,128)S(1)} %bitcast.12), channel_id=1, source_target_pairs={{0,1},{1,0},{2,3},{3,2},{4,5},{5,4},{6,7},{7,6},{8,9},{9,8},{10,11... | collective-permute-start | bytes 3538952 | tf_op jit(solution)/shard_map/ppermute | solution.py:381
  117.0 2.3 %collective-permute-done.1.other_ref = f32[2304,128]{1,0:T(8,128)S(1)} collective-permute-done((f32[2304,128]{1,0:T(8,128)S(1)}, f32[2304,128]{1,0:T(8,128)S(1)}, u32[]{:S(2)}, u32[]{:S(2)}) %collective-permute-start.1) | collective-permute-done | bytes 1179680 | tf_op jit(solution)/shard_map/ppermute | solution.py:381
  119.3 26.9 %factor.1 = (f32[64,1024]{1,0:T(8,128)}, f32[1,64]{1,0:T(1,128)}) custom-call(s32[2]{0:T(128)S(1)} %pad_add_fusion.where_ref, f32[2304,128]{1,0:T(8,128)S(1)} %bitcast.13, f32[2304,128]{1,0:T(8,128)S(1)} %collective-permute-done.1.other_ref), custom_call_target="tpu_custom_call" | custom-call | tf_op jit(solution)/shard_map/factor/pallas_call | solution.py:301
  (11 shorter events, 0.0 us)
Async XLA Ops:
  0.6 17.1 %copy-start = (f32[512,1024]{1,0:T(8,128)S(1)}, f32[512,1024]{1,0:T(8,128)}, u32[]{:S(2)}) copy-start(f32[512,1024]{1,0:T(8,128)} %design_ref.1) | copy-start | bytes 6291460
  3.9 13.8 %copy-start.1 = (f32[64,1152]{1,0:T(8,128)S(1)}, f32[64,1152]{1,0:T(8,128)}, u32[]{:S(2)}) copy-start(f32[64,1152]{1,0:T(8,128)} %arcs.1.after_ref) | copy-start | bytes 884740
  3.9 13.8 %copy-start.2 = (f32[512]{0:T(512)S(1)}, f32[512]{0:T(512)}, u32[]{:S(2)}) copy-start(f32[512]{0:T(512)} %param.8) | copy-start | bytes 6148
  3.9 13.8 %copy-start.3 = (f32[512]{0:T(512)S(1)}, f32[512]{0:T(512)}, u32[]{:S(2)}) copy-start(f32[512]{0:T(512)} %param.7) | copy-start | bytes 6148
  4.0 13.8 %copy-start.4 = (f32[64,1024]{1,0:T(8,128)S(1)}, f32[64,1024]{1,0:T(8,128)}, u32[]{:S(2)}) copy-start(f32[64,1024]{1,0:T(8,128)} %prior_ref.1) | copy-start | bytes 786436
  4.0 13.8 %copy-start.5 = (f32[64]{0:T(128)S(1)}, f32[64]{0:T(128)}, u32[]{:S(2)}) copy-start(f32[64]{0:T(128)} %param.11) | copy-start | bytes 772
  5.8 24.3 %all-to-all-start = ((f32[16,4,1152]{2,1,0:T(4,128)}), f32[16,4,1152]{2,1,0:T(4,128)}, u32[]{:S(2)}, u32[]{:S(2)}) async-start(f32[16,4,1152]{2,1,0:T(4,128)} %reshape.44), calls=%async_computation | async-start | bytes 589824 | tf_op jit(solution)/shard_map/all_to_all | solution.py:348
  22.5 8.6 %collective-permute-start = (f32[2304,128]{1,0:T(8,128)}, f32[2304,128]{1,0:T(8,128)}, u32[]{:S(2)}, u32[]{:S(2)}) collective-permute-start(f32[2304,128]{1,0:T(8,128)} %get-tuple-element.11), channel_id=1, source_target_pairs={{0,1},{1,0},{2,3},{3,2},{4,5},{5,4},{6,7},{7,6},{8,9},{9,8},{10,11... | collective-permute-start | bytes 3538952 | tf_op jit(solution)/shard_map/ppermute | solution.py:369
  110.2 9.1 %collective-permute-start.1 = (f32[2304,128]{1,0:T(8,128)S(1)}, f32[2304,128]{1,0:T(8,128)S(1)}, u32[]{:S(2)}, u32[]{:S(2)}) collective-permute-start(f32[2304,128]{1,0:T(8,128)S(1)} %bitcast.12), channel_id=1, source_target_pairs={{0,1},{1,0},{2,3},{3,2},{4,5},{5,4},{6,7},{7,6},{8,9},{9,8},{10,11... | collective-permute-start | bytes 3538952 | tf_op jit(solution)/shard_map/ppermute | solution.py:381

commit v3 on v2

--- a/solution.py
+++ b/solution.py
@@ -147,7 +147,8 @@
 
 def arcs_kernel(design_hbm, weight_hbm, obs_hbm, arc_hbm, out_ref, design_ref, weight_ref, obs_ref, arc_ref, sem):
     rows, width = design_ref.shape
-    arcs = out_ref.shape[0]
+    pieces, each = out_ref.shape[:2]
+    arcs = pieces * each // 2
     parts = row_parts(rows)
     copies = fetch(
         [(weight_hbm, weight_ref), (arc_hbm, arc_ref), (obs_hbm, obs_ref)]
@@ -157,18 +158,21 @@
     for copy in copies[:3]:
         copy.wait()
     w = weight_ref[...]
-    row = lax.broadcasted_iota(jnp.int32, (arcs, rows), 0)
-    member = jnp.where((row // 8) * 4 + row % 4 == arc_ref[...], w * w, 0.0)
+    number = lax.broadcasted_iota(jnp.int32, (arcs, rows), 0)
+    member = jnp.where(number == arc_ref[...], w * w, 0.0)
     total = jnp.sum(member, axis=1, keepdims=True)
     obs = jnp.sum(member * obs_ref[...], axis=1, keepdims=True)
     lane = lax.broadcasted_iota(jnp.int32, (arcs, NB), 1)
-    out_ref[:, width:] = jnp.where(lane == 0, obs, jnp.where(lane == 1, total, 0.0))
+    tail = jnp.where(lane == 0, obs, jnp.where(lane == 1, total, 0.0))
     sums = None
     for n, p in enumerate(parts):
         copies[3 + n].wait()
         more = exact(member[:, n * NB:(n + 1) * NB], design_ref[p, :])
         sums = more if sums is None else sums + more
-    out_ref[:, :width] = sums
+    sums = jnp.concatenate([sums, tail], axis=1)
+    for n in range(pieces):
+        at = n // 2 * each
+        out_ref[n] = sums[at:at + each]
 
 
 def half_kernel(mine, where_ref, tall_ref, flat_ref, p_ref, out_ref):
@@ -237,18 +241,17 @@
 
 
 def pair_kernel(where_ref, mine_ref, got_ref, arcs_ref, out_ref):
-    width = arcs_ref.shape[1] - NB
+    width = arcs_ref.shape[2] - NB
     nblk = width // NB
     order = blocks_of(nblk)
     half = len(order) // 2
     core = where_ref[0]
-    s = arcs_ref[0:8, :]
-    for r in range(8, arcs_ref.shape[0], 8):
-        s = s + arcs_ref[r:r + 8, :]
-    s = s + pltpu.roll(s, 4, 0)
+    s = arcs_ref[0]
+    for r in range(1, arcs_ref.shape[0]):
+        s = s + arcs_ref[r]
+    s = jnp.concatenate([s, jnp.zeros((8 - s.shape[0], s.shape[1]), f32)], axis=0)
     total = s[:, width + 1:width + 2] + bias_prior
-    sub = lax.broadcasted_iota(jnp.int32, s.shape, 0)
-    b = jnp.where(sub < 4, s * lax.rsqrt(jnp.broadcast_to(total, s.shape)), 0.0)
+    b = s * lax.rsqrt(jnp.broadcast_to(total, s.shape))
     obs = b[:, width:width + 1]
     p = jnp.sum(b[:, :width] * obs, axis=0, keepdims=True)
     h = b.astype(bf16).astype(f32)
@@ -317,12 +320,12 @@
 def on_device(design, observed, row_weight, arc_of_row, prior_factor, prior_rhs):
     rows, width = design.shape
     prows = prior_factor.shape[0]
-    nx, ny, nz, nc = (lax.axis_size(a) for a in ("x", "y", "z", "core"))
-    core, z = lax.axis_index("core"), lax.axis_index("z")
+    nz, nc = lax.axis_size(("zh", "zl")), lax.axis_size("core")
+    core, z = lax.axis_index("core"), lax.axis_index(("zh", "zl"))
     arcs = 2 * nz * nc
     nblk = width // NB
     half = len(blocks_of(nblk)) // 2 * NB
-    include = ((lax.axis_index("x") == 0) & (lax.axis_index("y") == 0)).astype(jnp.int32)
+    include = (lax.axis_index(("x", "yh", "yl")) == 0).astype(jnp.int32)
     weight = row_weight.reshape(1, rows)
     obs = observed.reshape(1, rows)
     arc = arc_of_row.reshape(1, rows)
@@ -334,7 +337,7 @@
         "arcs",
         None,
         (design, weight, obs, arc),
-        like(2 * arcs, width + NB),
+        like(nz * nc, 2 * nc, width + NB),
         [
             pltpu.VMEM((rows, width), f32),
             pltpu.VMEM((1, rows), f32),
@@ -345,7 +348,7 @@
         56,
         far=True,
     )
-    owned = lax.all_to_all(partial.reshape(nz * nc, 2 * nc, width + NB), ("z", "core"), 0, 0, tiled=True)
+    owned = lax.all_to_all(partial, ("zh", "zl", "core"), 0, 0, tiled=True)
     work = pl.CostEstimate(flops=2 * 10**11, bytes_accessed=10**7, transcendentals=0)
     send, tall, flat, p = call(
         first_kernel,
@@ -369,14 +372,15 @@
     got = lax.ppermute(send, "core", swap)
     where = jnp.stack([core, z * nc + core]).astype(jnp.int32)
     v = call(
-        pair_kernel, "pair", where, (keep, got, owned.reshape(-1, width + NB)), like(half, NB), [], 32
-    )
-    v = lax.all_to_all(v.reshape(nx, half // nx, NB), "x", 0, 0, tiled=True).sum(0)
-    plane = ny * nz
-    v = lax.all_to_all(v.reshape(plane, 1, v.size // plane), ("y", "z"), 0, 0, tiled=True).sum(0)
-    v = lax.all_to_all(jnp.broadcast_to(v, (plane, *v.shape)), ("y", "z"), 0, 0, tiled=True)
-    v = v.reshape(half // nx, NB)
-    v = lax.all_to_all(jnp.broadcast_to(v, (nx, *v.shape)), "x", 0, 0, tiled=True)
+        pair_kernel, "pair", where, (keep, got, owned), like(half, NB), [], 32
+    )
+    block, blocks = ("x", "yl", "zl"), ("yh", "zh")
+    nb, nbs = lax.axis_size(block), lax.axis_size(blocks)
+    v = lax.all_to_all(v.reshape(nb, half // nb, NB), block, 0, 0, tiled=True).sum(0)
+    v = lax.all_to_all(v.reshape(nbs, 1, v.size // nbs), blocks, 0, 0, tiled=True).sum(0)
+    v = lax.all_to_all(jnp.broadcast_to(v, (nbs, *v.shape)), blocks, 0, 0, tiled=True)
+    v = v.reshape(half // nb, NB)
+    v = lax.all_to_all(jnp.broadcast_to(v, (nb, *v.shape)), block, 0, 0, tiled=True)
     v = v.reshape(half, NB)
     other = lax.ppermute(v, "core", swap)
     factor, rhs = call(
@@ -392,20 +396,14 @@
 
 
 def solution(mesh):
-    fine = Mesh(mesh.devices.reshape(4, 8, 8, 2), ("x", "y", "z", "core"))
-    every = ("x", "y", "z", "core")
-    placed = (
-        P(every, None),
-        P(every),
-        P(every),
-        P(every, None),
-        P(("z", "core"), None),
-        P(("z", "core")),
-    )
+    fine = Mesh(mesh.devices.reshape(4, 4, 2, 4, 2, 2), ("x", "yh", "yl", "zh", "zl", "core"))
+    dev = ("zh", "zl", "core")
+    every = ("x", "yh", "yl") + dev
+    placed = (P(every, None), P(every), P(every), P(every, None), P(dev, None), P(dev))
     return jax.shard_map(
         on_device,
         mesh=fine,
         in_specs=placed,
-        out_specs=(P(("z", "core"), None), P(("z", "core"))),
+        out_specs=(P(dev, None), P(dev)),
         check_vma=False,
     )

time: 147 us -> 141 us (0.959)
  blocking collectives: 76.7 us -> 73.4 us
  local copies, waits for them, and re-layouts: 3.14 us -> 1.09 us
    all_to_all x4, blocking collectives: 76.7 us -> 73.4 us  [the longest x1 22.3 us: on_device(): lax.all_to_all(v.reshape(nb, half // nb, NB), block, 0, 0, tiled=True)]
    reshape x2 -> x0, local copies, waits for them, and re-layouts: 2.88 us -> none  [the longest x1 1.81 us: on_device(): partial.reshape(nz * nc, 2 * nc, width + NB)]
  transfers between devices with their start and end apart: 3 -> 3, of which waited for: 2 -> 2; matrix products, arithmetic and copies ran while one was open for 1% -> 0% of each run, Pallas kernels for 5% -> 5%
where the time goes in v3:
time: 141 us; the launch traced here: 140 us
  blocking collectives  73.4 us (52%)
  Pallas kernels  39 us (28%)
  starting transfers between devices  21.3 us (15%)
  waiting for transfers between devices  4.37 us (3%)
    pallas_call x5, Pallas kernels, call(): pl.pallas_call(kernel, out_shape=outs, in_specs=([SMEM] if where is not N...  39 us
    all_to_all x1, blocking collectives, on_device(): lax.all_to_all(v.reshape(nb, half // nb, NB), block, 0, 0, tiled=True)  22.3 us
    all_to_all x1, blocking collectives, on_device(): lax.all_to_all(v.reshape(nbs, 1, v.size // nbs), blocks, 0, 0, tiled=True)  20.5 us
    all_to_all x1, blocking collectives, on_device(): lax.all_to_all(jnp.broadcast_to(v, (nb, *v.shape)), block, 0, 0, tiled=True)  16.8 us
    all_to_all x1, blocking collectives, on_device(): lax.all_to_all(jnp.broadcast_to(v, (nbs, *v.shape)), blocks, 0, 0, tiled=...  14 us
    all_to_all x1, starting transfers between devices, on_device(): owned = lax.all_to_all(partial, ('zh', 'zl', 'core'), 0, 0, tiled=True)  11.8 us
    ppermute x1, starting transfers between devices, on_device(): other = lax.ppermute(v, 'core', swap)  7.26 us
  transfers between devices with their start and end apart: 3, of which 2 were waited for; matrix products, arithmetic and copies ran while one was open for 0% of the time, Pallas kernels for 5%

profile of v3, /device:TPU:1, one launch (start us, length us, event | category | flops | bytes accessed | tf_op | source)
XLA Modules:
  0.0 140.2 jit_solution(5465405225588990261)
XLA Ops:
  0.7 3.2 %arcs.1.after_ref = f32[16,4,1152]{2,1,0:T(4,128)} custom-call(f32[512,1024]{1,0:T(8,128)} %design_ref.1, f32[1,512]{1,0:T(1,128)} %bitcast.15, f32[1,512]{1,0:T(1,128)} %bitcast.17, s32[1,512]{1,0:T(1,128)} %bitcast.22), custom_call_target="tpu_custom_call" | custom-call | tf_op jit(solution)/shard_map/arcs/pallas_call | solution.py:304
  3.9 11.8 %all-to-all-start = ((f32[16,4,1152]{2,1,0:T(4,128)}), f32[16,4,1152]{2,1,0:T(4,128)}, u32[]{:S(2)}, u32[]{:S(2)}) async-start(f32[16,4,1152]{2,1,0:T(4,128)} %arcs.1.after_ref), calls=%async_computation | async-start | bytes 589824 | tf_op jit(solution)/shard_map/all_to_all | solution.py:351
  15.8 0.1 pad_add_fusion.1.where_ref
  15.9 0.0 copy-done
  15.9 0.0 copy-done.5
  15.9 0.0 copy-start.1
  15.9 1.0 copy-done.1
  16.8 4.8 %first.1 = (f32[2304,128]{1,0:T(8,128)}, bf16[1024,1280]{1,0:T(8,128)(2,1)S(1)}, bf16[1280,1024]{1,0:T(8,128)(2,1)S(1)}, f32[8,1024]{1,0:T(8,128)S(1)}) custom-call(s32[2]{0:T(128)S(1)} %pad_add_fusion.1.where_ref, f32[512,1024]{1,0:T(8,128)S(1)} %copy-done, f32[1,512]{1,0:T(1,128)S(1)} %bitcast.16, f32[1,512]{1,0:T(1,128)S(1)} %bitcast.18, ...), custom_call_target="tpu_custom_call" | custom-call | flops 199999995904 | bytes 10000000 | tf_op jit(solution)/shard_map/first/pallas_call | solution.py:304
  21.6 2.2 %collective-permute-start = (f32[2304,128]{1,0:T(8,128)}, f32[2304,128]{1,0:T(8,128)}, u32[]{:S(2)}, u32[]{:S(2)}) collective-permute-start(f32[2304,128]{1,0:T(8,128)} %get-tuple-element.11), channel_id=1, source_target_pairs={{0,1},{1,0},{2,3},{3,2},{4,5},{5,4},{6,7},{7,6},{8,9},{9,8},{10,11... | collective-permute-start | bytes 3538952 | tf_op jit(solution)/shard_map/ppermute | solution.py:372
  23.8 2.2 %keep.1.mine_ref = f32[2304,128]{1,0:T(8,128)S(1)} custom-call(s32[2]{0:T(128)S(1)} %pad_add_fusion.1.where_ref, bf16[1024,1280]{1,0:T(8,128)(2,1)S(1)} %get-tuple-element.8.tall_ref, bf16[1280,1024]{1,0:T(8,128)(2,1)S(1)} %get-tuple-element.9.flat_ref, f32[8,1024]{1,0:T(8,128)S(1)} %get-tuple-element.10.p_ref), custom_call_target="tpu_custom_call" | custom-call | flops 199999995904 | bytes 10000000 | tf_op jit(solution)/shard_map/keep/pallas_call | solution.py:304
  26.1 0.1 pad_add_fusion.where_ref
  26.2 2.1 %all-to-all-done.arcs_ref = f32[16,4,1152]{2,1,0:T(4,128)} async-done(((f32[16,4,1152]{2,1,0:T(4,128)}), f32[16,4,1152]{2,1,0:T(4,128)}, u32[]{:S(2)}, u32[]{:S(2)}) %all-to-all-start) | async-done | bytes 294944 | tf_op jit(solution)/shard_map/all_to_all | solution.py:351
  28.3 0.0 collective-permute-done.got_ref
  28.3 1.8 %pair.1 = f32[2304,128]{1,0:T(8,128)S(1)} custom-call(s32[2]{0:T(128)S(1)} %pad_add_fusion.where_ref, f32[2304,128]{1,0:T(8,128)S(1)} %keep.1.mine_ref, f32[2304,128]{1,0:T(8,128)} %collective-permute-done.got_ref, f32[16,4,1152]{2,1,0:T(4,128)} %all-to-all-done.arcs_ref), custom_call_target="tpu_custom_call" | custom-call | tf_op jit(solution)/shard_map/pair/pallas_call | solution.py:304
  30.1 22.3 %all_to_all.25 = f32[16,144,128]{2,1,0:T(8,128)S(1)} all-to-all(f32[16,144,128]{2,1,0:T(8,128)S(1)} %bitcast.14), channel_id=1, replica_groups=mesh['x'=4,'yh'=4,'yl'=2,'zh'=4,'zl'=2,'core'=2] {'x','yl','zl'}, dimensions={0} | all-to-all | bytes 2359296 | tf_op jit(solution)/shard_map/all_to_all | solution.py:379
  52.4 0.1 reduce_sum.18
  52.4 20.5 %all_to_all.26 = f32[16,1,1152]{2,1,0:T(1,128)S(1)} all-to-all(f32[16,1,1152]{2,1,0:T(1,128)S(1)} %bitcast.20), channel_id=1, replica_groups=mesh['x'=4,'yh'=4,'yl'=2,'zh'=4,'zl'=2,'core'=2] {'yh','zh'}, dimensions={0} | all-to-all | bytes 147456 | tf_op jit(solution)/shard_map/all_to_all | solution.py:380
  72.9 0.1 reduce_sum.19
  73.0 14.0 %all_to_all.27 = f32[16,1,1152]{2,1,0:T(1,128)S(1)} all-to-all(f32[16,1,1152]{2,1,0:T(1,128)S(1)} %broadcast_in_dim.6), channel_id=1, replica_groups=mesh['x'=4,'yh'=4,'yl'=2,'zh'=4,'zl'=2,'core'=2] {'yh','zh'}, dimensions={0} | all-to-all | bytes 147456 | tf_op jit(solution)/shard_map/all_to_all | solution.py:381
  87.0 0.1 broadcast_in_dim.7
  87.0 16.8 %all_to_all.28 = f32[16,144,128]{2,1,0:T(8,128)S(1)} all-to-all(f32[16,144,128]{2,1,0:T(8,128)S(1)} %broadcast_in_dim.7), channel_id=1, replica_groups=mesh['x'=4,'yh'=4,'yl'=2,'zh'=4,'zl'=2,'core'=2] {'x','yl','zl'}, dimensions={0} | all-to-all | bytes 2359296 | tf_op jit(solution)/shard_map/all_to_all | solution.py:383
  103.8 7.3 %collective-permute-start.1 = (f32[2304,128]{1,0:T(8,128)S(1)}, f32[2304,128]{1,0:T(8,128)S(1)}, u32[]{:S(2)}, u32[]{:S(2)}) collective-permute-start(f32[2304,128]{1,0:T(8,128)S(1)} %bitcast.12), channel_id=1, source_target_pairs={{0,1},{1,0},{2,3},{3,2},{4,5},{5,4},{6,7},{7,6},{8,9},{9,8},{10,11... | collective-permute-start | bytes 3538952 | tf_op jit(solution)/shard_map/ppermute | solution.py:385
  111.1 2.3 %collective-permute-done.1.other_ref = f32[2304,128]{1,0:T(8,128)S(1)} collective-permute-done((f32[2304,128]{1,0:T(8,128)S(1)}, f32[2304,128]{1,0:T(8,128)S(1)}, u32[]{:S(2)}, u32[]{:S(2)}) %collective-permute-start.1) | collective-permute-done | bytes 1179680 | tf_op jit(solution)/shard_map/ppermute | solution.py:385
  113.3 26.9 %factor.1 = (f32[64,1024]{1,0:T(8,128)}, f32[1,64]{1,0:T(1,128)}) custom-call(s32[2]{0:T(128)S(1)} %pad_add_fusion.where_ref, f32[2304,128]{1,0:T(8,128)S(1)} %bitcast.13, f32[2304,128]{1,0:T(8,128)S(1)} %collective-permute-done.1.other_ref), custom_call_target="tpu_custom_call" | custom-call | tf_op jit(solution)/shard_map/factor/pallas_call | solution.py:304
  (9 shorter events, 0.1 us)
Async XLA Ops:
  0.6 15.2 %copy-start = (f32[512,1024]{1,0:T(8,128)S(1)}, f32[512,1024]{1,0:T(8,128)}, u32[]{:S(2)}) copy-start(f32[512,1024]{1,0:T(8,128)} %design_ref.1) | copy-start | bytes 6291460
  0.6 15.2 %copy-start.2 = (f32[512]{0:T(512)S(1)}, f32[512]{0:T(512)}, u32[]{:S(2)}) copy-start(f32[512]{0:T(512)} %param.8) | copy-start | bytes 6148
  0.7 15.2 %copy-start.3 = (f32[512]{0:T(512)S(1)}, f32[512]{0:T(512)}, u32[]{:S(2)}) copy-start(f32[512]{0:T(512)} %param.7) | copy-start | bytes 6148
  0.7 15.2 %copy-start.4 = (f32[64,1024]{1,0:T(8,128)S(1)}, f32[64,1024]{1,0:T(8,128)}, u32[]{:S(2)}) copy-start(f32[64,1024]{1,0:T(8,128)} %prior_ref.1) | copy-start | bytes 786436
  0.7 15.2 %copy-start.5 = (f32[64]{0:T(128)S(1)}, f32[64]{0:T(128)}, u32[]{:S(2)}) copy-start(f32[64]{0:T(128)} %param.11) | copy-start | bytes 772
  3.9 24.3 %all-to-all-start = ((f32[16,4,1152]{2,1,0:T(4,128)}), f32[16,4,1152]{2,1,0:T(4,128)}, u32[]{:S(2)}, u32[]{:S(2)}) async-start(f32[16,4,1152]{2,1,0:T(4,128)} %arcs.1.after_ref), calls=%async_computation | async-start | bytes 589824 | tf_op jit(solution)/shard_map/all_to_all | solution.py:351
  15.9 1.0 copy-start.1
  21.6 6.6 %collective-permute-start = (f32[2304,128]{1,0:T(8,128)}, f32[2304,128]{1,0:T(8,128)}, u32[]{:S(2)}, u32[]{:S(2)}) collective-permute-start(f32[2304,128]{1,0:T(8,128)} %get-tuple-element.11), channel_id=1, source_target_pairs={{0,1},{1,0},{2,3},{3,2},{4,5},{5,4},{6,7},{7,6},{8,9},{9,8},{10,11... | collective-permute-start | bytes 3538952 | tf_op jit(solution)/shard_map/ppermute | solution.py:372
  103.8 9.5 %collective-permute-start.1 = (f32[2304,128]{1,0:T(8,128)S(1)}, f32[2304,128]{1,0:T(8,128)S(1)}, u32[]{:S(2)}, u32[]{:S(2)}) collective-permute-start(f32[2304,128]{1,0:T(8,128)S(1)} %bitcast.12), channel_id=1, source_target_pairs={{0,1},{1,0},{2,3},{3,2},{4,5},{5,4},{6,7},{7,6},{8,9},{9,8},{10,11... | collective-permute-start | bytes 3538952 | tf_op jit(solution)/shard_map/ppermute | solution.py:385

commit v4 on v3

--- a/solution.py
+++ b/solution.py
@@ -145,7 +145,7 @@
     return [pl.ds(r, NB) for r in range(0, rows, NB)]
 
 
-def arcs_kernel(design_hbm, weight_hbm, obs_hbm, arc_hbm, out_ref, design_ref, weight_ref, obs_ref, arc_ref, sem):
+def arcs_kernel(design_hbm, weight_hbm, obs_hbm, arc_hbm, out_ref, done_ref, design_ref, weight_ref, obs_ref, arc_ref, sem):
     rows, width = design_ref.shape
     pieces, each = out_ref.shape[:2]
     arcs = pieces * each // 2
@@ -157,6 +157,7 @@
     )
     for copy in copies[:3]:
         copy.wait()
+    done_ref[...] = jnp.zeros_like(done_ref)
     w = weight_ref[...]
     number = lax.broadcasted_iota(jnp.int32, (arcs, rows), 0)
     member = jnp.where(number == arc_ref[...], w * w, 0.0)
@@ -332,12 +333,12 @@
     nparts = rows // NB
     deep = rows + NB
     here = jnp.stack([core, include]).astype(jnp.int32)
-    partial = call(
+    partial, done = call(
         arcs_kernel,
         "arcs",
         None,
         (design, weight, obs, arc),
-        like(nz * nc, 2 * nc, width + NB),
+        (like(nz * nc, 2 * nc, width + NB), like(8, NB)),
         [
             pltpu.VMEM((rows, width), f32),
             pltpu.VMEM((1, rows), f32),
@@ -354,7 +355,7 @@
         first_kernel,
         "first",
         here,
-        (design, weight, obs, prior_factor, prior_rhs.reshape(1, prows), partial),
+        (design, weight, obs, prior_factor, prior_rhs.reshape(1, prows), done),
         (
             like(half, NB),
             pltpu.VMEM((width, 2 * deep), bf16),
@@ -374,11 +375,12 @@
     v = call(
         pair_kernel, "pair", where, (keep, got, owned), like(half, NB), [], 32
     )
-    block, blocks = ("x", "yl", "zl"), ("yh", "zh")
-    nb, nbs = lax.axis_size(block), lax.axis_size(blocks)
+    block = ("x", "yl", "zl")
+    nb, ny, nzh = (lax.axis_size(a) for a in (block, "yh", "zh"))
     v = lax.all_to_all(v.reshape(nb, half // nb, NB), block, 0, 0, tiled=True).sum(0)
-    v = lax.all_to_all(v.reshape(nbs, 1, v.size // nbs), blocks, 0, 0, tiled=True).sum(0)
-    v = lax.all_to_all(jnp.broadcast_to(v, (nbs, *v.shape)), blocks, 0, 0, tiled=True)
+    v = lax.all_to_all(v.reshape(ny, 1, v.size // ny), "yh", 0, 0, tiled=True).sum(0)
+    v = lax.all_to_all(jnp.broadcast_to(v, (nzh, *v.shape)), "zh", 0, 0, tiled=True).sum(0)
+    v = lax.all_to_all(jnp.broadcast_to(v, (ny, *v.shape)), "yh", 0, 0, tiled=True)
     v = v.reshape(half // nb, NB)
     v = lax.all_to_all(jnp.broadcast_to(v, (nb, *v.shape)), block, 0, 0, tiled=True)
     v = v.reshape(half, NB)

time: 141 us -> 140 us (level)
  blocking collectives: 73.4 us -> 71 us
  starting transfers between devices: 21.3 us -> 23.1 us
    ppermute x1, starting transfers between devices: 7.26 us -> 9.05 us  [on_device(): other = lax.ppermute(v, 'core', swap)]
    all_to_all x2 -> x3, blocking collectives: 34.4 us -> 33 us  [the longest x1 12.7 us: on_device(): lax.all_to_all(v.reshape(ny, 1, v.size // ny), 'yh', 0, 0, tiled=True)]
where the time goes in v4:
time: 140 us
  blocking collectives  71 us (51%)
  Pallas kernels  39 us (28%)
  starting transfers between devices  23.1 us (16%)
  waiting for transfers between devices  4.64 us (3%)
    pallas_call x5, Pallas kernels, call(): pl.pallas_call(kernel, out_shape=outs, in_specs=([SMEM] if where is not N...  39 us
    all_to_all x1, blocking collectives, on_device(): lax.all_to_all(v.reshape(nb, half // nb, NB), block, 0, 0, tiled=True)  22.6 us
    all_to_all x1, blocking collectives, on_device(): lax.all_to_all(jnp.broadcast_to(v, (nb, *v.shape)), block, 0, 0, tiled=True)  15.4 us
    all_to_all x1, blocking collectives, on_device(): lax.all_to_all(v.reshape(ny, 1, v.size // ny), 'yh', 0, 0, tiled=True)  12.7 us
    all_to_all x1, starting transfers between devices, on_device(): owned = lax.all_to_all(partial, ('zh', 'zl', 'core'), 0, 0, tiled=True)  11.8 us
    all_to_all x1, blocking collectives, on_device(): lax.all_to_all(jnp.broadcast_to(v, (nzh, *v.shape)), 'zh', 0, 0, tiled=True)  11 us
    all_to_all x1, blocking collectives, on_device(): lax.all_to_all(jnp.broadcast_to(v, (ny, *v.shape)), 'yh', 0, 0, tiled=True)  9.3 us
    ppermute x1, starting transfers between devices, on_device(): other = lax.ppermute(v, 'core', swap)  9.05 us
  transfers between devices with their start and end apart: 3, of which 2 were waited for; matrix products, arithmetic and copies ran while one was open for 0% of the time, Pallas kernels for 5%

profile of v4, /device:TPU:1, one launch (start us, length us, event | category | flops | bytes accessed | tf_op | source)
XLA Modules:
  0.0 139.8 jit_solution(4726508486369824731)
XLA Ops:
  0.7 3.2 %arcs.1 = (f32[16,4,1152]{2,1,0:T(4,128)}, f32[8,128]{1,0:T(8,128)}) custom-call(f32[512,1024]{1,0:T(8,128)} %design_ref.1, f32[1,512]{1,0:T(1,128)} %bitcast.15, f32[1,512]{1,0:T(1,128)} %bitcast.17, s32[1,512]{1,0:T(1,128)} %bitcast.22), custom_call_target="tpu_custom_call" | custom-call | tf_op jit(solution)/shard_map/arcs/pallas_call | solution.py:305
  3.9 11.8 %all-to-all-start = ((f32[16,4,1152]{2,1,0:T(4,128)}), f32[16,4,1152]{2,1,0:T(4,128)}, u32[]{:S(2)}, u32[]{:S(2)}) async-start(f32[16,4,1152]{2,1,0:T(4,128)} %get-tuple-element.15), calls=%async_computation | async-start | bytes 589824 | tf_op jit(solution)/shard_map/all_to_all | solution.py:352
  15.8 0.1 pad_add_fusion.1.where_ref
  15.9 0.0 copy-start.4
  15.9 0.7 copy-done.4
  16.6 4.8 %first.1 = (f32[2304,128]{1,0:T(8,128)}, bf16[1024,1280]{1,0:T(8,128)(2,1)S(1)}, bf16[1280,1024]{1,0:T(8,128)(2,1)S(1)}, f32[8,1024]{1,0:T(8,128)S(1)}) custom-call(s32[2]{0:T(128)S(1)} %pad_add_fusion.1.where_ref, f32[512,1024]{1,0:T(8,128)S(1)} %copy-done, f32[1,512]{1,0:T(1,128)S(1)} %bitcast.16, f32[1,512]{1,0:T(1,128)S(1)} %bitcast.18, ...), custom_call_target="tpu_custom_call" | custom-call | flops 199999995904 | bytes 10000000 | tf_op jit(solution)/shard_map/first/pallas_call | solution.py:305
  21.4 2.2 %collective-permute-start = (f32[2304,128]{1,0:T(8,128)}, f32[2304,128]{1,0:T(8,128)}, u32[]{:S(2)}, u32[]{:S(2)}) collective-permute-start(f32[2304,128]{1,0:T(8,128)} %get-tuple-element.14), channel_id=1, source_target_pairs={{0,1},{1,0},{2,3},{3,2},{4,5},{5,4},{6,7},{7,6},{8,9},{9,8},{10,11... | collective-permute-start | bytes 3538952 | tf_op jit(solution)/shard_map/ppermute | solution.py:373
  23.6 2.2 %keep.1.mine_ref = f32[2304,128]{1,0:T(8,128)S(1)} custom-call(s32[2]{0:T(128)S(1)} %pad_add_fusion.1.where_ref, bf16[1024,1280]{1,0:T(8,128)(2,1)S(1)} %get-tuple-element.11.tall_ref, bf16[1280,1024]{1,0:T(8,128)(2,1)S(1)} %get-tuple-element.12.flat_ref, f32[8,1024]{1,0:T(8,128)S(1)} %get-tuple-element.13.p_ref), custom_call_target="tpu_custom_call" | custom-call | flops 199999995904 | bytes 10000000 | tf_op jit(solution)/shard_map/keep/pallas_call | solution.py:305
  25.8 0.1 pad_add_fusion.where_ref
  25.9 2.4 %all-to-all-done.arcs_ref = f32[16,4,1152]{2,1,0:T(4,128)} async-done(((f32[16,4,1152]{2,1,0:T(4,128)}), f32[16,4,1152]{2,1,0:T(4,128)}, u32[]{:S(2)}, u32[]{:S(2)}) %all-to-all-start) | async-done | bytes 294944 | tf_op jit(solution)/shard_map/all_to_all | solution.py:352
  28.3 0.0 collective-permute-done.got_ref
  28.3 1.8 %pair.1 = f32[2304,128]{1,0:T(8,128)S(1)} custom-call(s32[2]{0:T(128)S(1)} %pad_add_fusion.where_ref, f32[2304,128]{1,0:T(8,128)S(1)} %keep.1.mine_ref, f32[2304,128]{1,0:T(8,128)} %collective-permute-done.got_ref, f32[16,4,1152]{2,1,0:T(4,128)} %all-to-all-done.arcs_ref), custom_call_target="tpu_custom_call" | custom-call | tf_op jit(solution)/shard_map/pair/pallas_call | solution.py:305
  30.1 22.6 %all_to_all.30 = f32[16,144,128]{2,1,0:T(8,128)S(1)} all-to-all(f32[16,144,128]{2,1,0:T(8,128)S(1)} %bitcast.14), channel_id=1, replica_groups=mesh['x'=4,'yh'=4,'yl'=2,'zh'=4,'zl'=2,'core'=2] {'x','yl','zl'}, dimensions={0} | all-to-all | bytes 2359296 | tf_op jit(solution)/shard_map/all_to_all | solution.py:380
  52.7 0.1 reduce_sum.27
  52.7 12.7 %all_to_all.31 = f32[4,1,4608]{2,1,0:T(1,128)S(1)} all-to-all(f32[4,1,4608]{2,1,0:T(1,128)S(1)} %bitcast.20), channel_id=1, replica_groups=mesh['x'=4,'yh'=4,'yl'=2,'zh'=4,'zl'=2,'core'=2] {'yh'}, dimensions={0} | all-to-all | bytes 147456 | tf_op jit(solution)/shard_map/all_to_all | solution.py:381
  65.5 0.1 reduce_sum.28
  65.6 11.0 %all_to_all.32 = f32[4,1,4608]{2,1,0:T(1,128)S(1)} all-to-all(f32[4,1,4608]{2,1,0:T(1,128)S(1)} %broadcast_in_dim.9), channel_id=1, replica_groups=mesh['x'=4,'yh'=4,'yl'=2,'zh'=4,'zl'=2,'core'=2] {'zh'}, dimensions={0} | all-to-all | bytes 147456 | tf_op jit(solution)/shard_map/all_to_all | solution.py:382
  76.6 0.1 reduce_sum.29
  76.7 9.3 %all_to_all.33 = f32[4,1,4608]{2,1,0:T(1,128)S(1)} all-to-all(f32[4,1,4608]{2,1,0:T(1,128)S(1)} %broadcast_in_dim.10), channel_id=1, replica_groups=mesh['x'=4,'yh'=4,'yl'=2,'zh'=4,'zl'=2,'core'=2] {'yh'}, dimensions={0} | all-to-all | bytes 147456 | tf_op jit(solution)/shard_map/all_to_all | solution.py:383
  86.0 0.1 broadcast_in_dim.11
  86.1 15.4 %all_to_all.34 = f32[16,144,128]{2,1,0:T(8,128)S(1)} all-to-all(f32[16,144,128]{2,1,0:T(8,128)S(1)} %broadcast_in_dim.11), channel_id=1, replica_groups=mesh['x'=4,'yh'=4,'yl'=2,'zh'=4,'zl'=2,'core'=2] {'x','yl','zl'}, dimensions={0} | all-to-all | bytes 2359296 | tf_op jit(solution)/shard_map/all_to_all | solution.py:385
  101.5 9.1 %collective-permute-start.1 = (f32[2304,128]{1,0:T(8,128)S(1)}, f32[2304,128]{1,0:T(8,128)S(1)}, u32[]{:S(2)}, u32[]{:S(2)}) collective-permute-start(f32[2304,128]{1,0:T(8,128)S(1)} %bitcast.12), channel_id=1, source_target_pairs={{0,1},{1,0},{2,3},{3,2},{4,5},{5,4},{6,7},{7,6},{8,9},{9,8},{10,11... | collective-permute-start | bytes 3538952 | tf_op jit(solution)/shard_map/ppermute | solution.py:387
  110.6 2.3 %collective-permute-done.1.other_ref = f32[2304,128]{1,0:T(8,128)S(1)} collective-permute-done((f32[2304,128]{1,0:T(8,128)S(1)}, f32[2304,128]{1,0:T(8,128)S(1)}, u32[]{:S(2)}, u32[]{:S(2)}) %collective-permute-start.1) | collective-permute-done | bytes 1179680 | tf_op jit(solution)/shard_map/ppermute | solution.py:387
  112.9 26.9 %factor.1 = (f32[64,1024]{1,0:T(8,128)}, f32[1,64]{1,0:T(1,128)}) custom-call(s32[2]{0:T(128)S(1)} %pad_add_fusion.where_ref, f32[2304,128]{1,0:T(8,128)S(1)} %bitcast.13, f32[2304,128]{1,0:T(8,128)S(1)} %collective-permute-done.1.other_ref), custom_call_target="tpu_custom_call" | custom-call | tf_op jit(solution)/shard_map/factor/pallas_call | solution.py:305
  (12 shorter events, 0.1 us)
Async XLA Ops:
  0.6 15.2 %copy-start = (f32[512,1024]{1,0:T(8,128)S(1)}, f32[512,1024]{1,0:T(8,128)}, u32[]{:S(2)}) copy-start(f32[512,1024]{1,0:T(8,128)} %design_ref.1) | copy-start | bytes 6291460
  0.6 15.2 %copy-start.1 = (f32[512]{0:T(512)S(1)}, f32[512]{0:T(512)}, u32[]{:S(2)}) copy-start(f32[512]{0:T(512)} %param.8) | copy-start | bytes 6148
  0.7 15.2 %copy-start.2 = (f32[512]{0:T(512)S(1)}, f32[512]{0:T(512)}, u32[]{:S(2)}) copy-start(f32[512]{0:T(512)} %param.7) | copy-start | bytes 6148
  0.7 15.2 %copy-start.3 = (f32[64,1024]{1,0:T(8,128)S(1)}, f32[64,1024]{1,0:T(8,128)}, u32[]{:S(2)}) copy-start(f32[64,1024]{1,0:T(8,128)} %prior_ref.1) | copy-start | bytes 786436
  0.7 15.2 %copy-start.5 = (f32[64]{0:T(128)S(1)}, f32[64]{0:T(128)}, u32[]{:S(2)}) copy-start(f32[64]{0:T(128)} %param.11) | copy-start | bytes 772
  3.9 24.3 %all-to-all-start = ((f32[16,4,1152]{2,1,0:T(4,128)}), f32[16,4,1152]{2,1,0:T(4,128)}, u32[]{:S(2)}, u32[]{:S(2)}) async-start(f32[16,4,1152]{2,1,0:T(4,128)} %get-tuple-element.15), calls=%async_computation | async-start | bytes 589824 | tf_op jit(solution)/shard_map/all_to_all | solution.py:352
  15.9 0.7 copy-start.4
  21.4 6.9 %collective-permute-start = (f32[2304,128]{1,0:T(8,128)}, f32[2304,128]{1,0:T(8,128)}, u32[]{:S(2)}, u32[]{:S(2)}) collective-permute-start(f32[2304,128]{1,0:T(8,128)} %get-tuple-element.14), channel_id=1, source_target_pairs={{0,1},{1,0},{2,3},{3,2},{4,5},{5,4},{6,7},{7,6},{8,9},{9,8},{10,11... | collective-permute-start | bytes 3538952 | tf_op jit(solution)/shard_map/ppermute | solution.py:373
  101.5 11.3 %collective-permute-start.1 = (f32[2304,128]{1,0:T(8,128)S(1)}, f32[2304,128]{1,0:T(8,128)S(1)}, u32[]{:S(2)}, u32[]{:S(2)}) collective-permute-start(f32[2304,128]{1,0:T(8,128)S(1)} %bitcast.12), channel_id=1, source_target_pairs={{0,1},{1,0},{2,3},{3,2},{4,5},{5,4},{6,7},{7,6},{8,9},{9,8},{10,11... | collective-permute-start | bytes 3538952 | tf_op jit(solution)/shard_map/ppermute | solution.py:387

commit v5 on v4

--- a/solution.py
+++ b/solution.py
@@ -40,7 +40,7 @@
 def dot(a, b, ca, cb):
     return lax.dot_general(a, b, (((ca,), (cb,)), ((), ())), preferred_element_type=f32)
 
-def factor_block(rows, tall=2, ahead=2):
+def factor_block(rows, side=None, tall=2, ahead=2):
     sub = lax.broadcasted_iota(jnp.int32, (8, 128), 0)
     lane = lax.broadcasted_iota(jnp.int32, (8, 128), 1)
     n = 16
@@ -51,26 +51,34 @@
         near = list(range(b + tall, min(b + tall + ahead, n)))
         steps = 8 * tall
         col = [{c: across(left[c], 8 * b + j) for c in own[j // 8:] + near} for j in range(steps)]
+        if side is not None:
+            next(side, None)
         x = {c: left[c] for c in own}
         y = {c: jnp.where(lane == sub + 8 * c, 1.0, 0.0) for c in own}
         diag = {c: jnp.ones((8, 128), f32) for c in own}
-        mults = []
+        mults, heads, qs = [], {}, []
         for j in range(steps):
             home = own[j // 8]
             q = 1.0 / spread(col[j][home], j % 8)
             diag[home] = jnp.where(sub == j % 8, q, diag[home])
-            scaled = {c: col[j][c] * q for c in col[j]}
+            scaled = {c: col[j][c] * q for c in own[j // 8:]}
+            qs.append(q)
             for k in range(j + 1, steps):
                 kh = own[k // 8]
                 head = spread(col[j][kh], k % 8)
-                for c in col[k]:
+                heads[j, k] = head
+                for c in own[k // 8:]:
                     col[k][c] = col[k][c] - scaled[c] * head
             sx, sy = spread(x[home], j % 8), spread(y[home], j % 8)
             for c in own[j // 8:]:
                 m = jnp.where(sub > j % 8, scaled[c], 0.0) if c == home else scaled[c]
                 x[c] = x[c] - m * sx
                 y[c] = y[c] - m * sy
-            mults.append(scaled)
+        for j in range(steps):
+            mults.append({c: col[j][c] * qs[j] for c in near})
+            for k in range(j + 1, steps):
+                for c in near:
+                    col[k][c] = col[k][c] - mults[j][c] * heads[j, k]
         done = (lane >= 8 * b) & (lane < 8 * (b + tall))
         z = {c: jnp.where(done, y[c], x[c]) for c in own}
         if near:
@@ -98,30 +106,58 @@
                 left[c] = jnp.where(done, 0.0, left[c]) - upd[8 * c:8 * c + 8, :]
     return up, inv
 
+def strips(lo, hi):
+    spans = []
+    while lo < hi:
+        end = min(lo + 2 * NB - lo % (2 * NB), hi)
+        spans.append((lo, end))
+        lo = end
+    return spans
+
+
+def later_work(a_ref, out_ref, t, p, r0, n, width):
+    top = r0 + NB
+    turned = [left_stack(p.T, 1)]
+    flat = right_stack(p, 0)
+    pieces = []
+    for lo, hi in strips(top + NB, width):
+        q = dot(t, right_stack(a_ref[r0:top, lo:hi], 0), 1, 0)
+        out_ref[r0:top, lo:hi] = q
+        pieces.append((lo, hi, right_stack(q, 0)))
+        if lo < n:
+            turned.append(left_stack(q.T, 1))
+        yield
+    full = jnp.concatenate(turned, axis=0)
+    for lo, hi, q in pieces:
+        end = min(hi, n)
+        a_ref[top:end, lo:hi] = a_ref[top:end, lo:hi] - dot(full[:end - top], q, 1, 0)
+        yield
+
+
 def chol_body(a_ref, out_ref, nblk, width):
+    n = nblk * NB
+    li = lax.broadcasted_iota(jnp.int32, (NB, NB), 1)
+    si = lax.broadcasted_iota(jnp.int32, (NB, NB), 0)
+    side = None
     for k in range(nblk):
         r0 = k * NB
-        rows = [a_ref[r0 + 8*b: r0 + 8*b + 8, r0:r0 + NB] for b in range(16)]
-        up, inv = factor_block(rows)
-        li = lax.broadcasted_iota(jnp.int32, (NB, NB), 1)
-        si = lax.broadcasted_iota(jnp.int32, (NB, NB), 0)
+        rows = [a_ref[r0 + 8 * b:r0 + 8 * b + 8, r0:r0 + NB] for b in range(16)]
+        up, inv = factor_block(rows, side)
+        if side is not None:
+            for _ in side:
+                pass
         out_ref[r0:r0 + NB, r0:r0 + NB] = jnp.where(li >= si, jnp.concatenate(up, axis=0), 0.0)
-        t = left_stack(jnp.concatenate(inv, axis=0), 1)
         if r0 > 0:
             out_ref[r0:r0 + NB, 0:r0] = jnp.zeros((NB, r0), f32)
-        pieces = []
-        lo = r0 + NB
-        while lo < width:
-            hi = min(lo + 2 * NB - lo % (2 * NB), width)
-            p = dot(t, right_stack(a_ref[r0:r0 + NB, lo:hi], 0), 1, 0)
-            out_ref[r0:r0 + NB, lo:hi] = p
-            pieces.append((lo, hi, p))
-            lo = hi
+        t = left_stack(jnp.concatenate(inv, axis=0), 1)
+        top = r0 + NB
+        p = dot(t, right_stack(a_ref[r0:top, top:top + NB], 0), 1, 0)
+        out_ref[r0:top, top:top + NB] = p
         if k + 1 < nblk:
-            full = jnp.concatenate([left_stack(p.T, 1) for lo, hi, p in pieces if lo < nblk * NB], axis=0)
-            for lo, hi, p in pieces:
-                top, end = r0 + NB, min(hi, nblk * NB)
-                a_ref[top:end, lo:hi] = a_ref[top:end, lo:hi] - dot(full[:end - top], right_stack(p, 0), 1, 0)
+            a_ref[top:top + NB, top:top + NB] = a_ref[top:top + NB, top:top + NB] - dot(
+                left_stack(p.T, 1), right_stack(p, 0), 1, 0
+            )
+            side = later_work(a_ref, out_ref, t, p, r0, n, width)
 
 
 def exact(a, b):
@@ -379,9 +415,8 @@
     nb, ny, nzh = (lax.axis_size(a) for a in (block, "yh", "zh"))
     v = lax.all_to_all(v.reshape(nb, half // nb, NB), block, 0, 0, tiled=True).sum(0)
     v = lax.all_to_all(v.reshape(ny, 1, v.size // ny), "yh", 0, 0, tiled=True).sum(0)
-    v = lax.all_to_all(jnp.broadcast_to(v, (nzh, *v.shape)), "zh", 0, 0, tiled=True).sum(0)
-    v = lax.all_to_all(jnp.broadcast_to(v, (ny, *v.shape)), "yh", 0, 0, tiled=True)
-    v = v.reshape(half // nb, NB)
+    v = lax.all_to_all(jnp.broadcast_to(v, (ny * nzh, *v.shape)), ("yh", "zh"), 0, 0, tiled=True)
+    v = v.reshape(ny, nzh, 1, v.shape[-1]).sum(1).reshape(half // nb, NB)
     v = lax.all_to_all(jnp.broadcast_to(v, (nb, *v.shape)), block, 0, 0, tiled=True)
     v = v.reshape(half, NB)
     other = lax.ppermute(v, "core", swap)

time: 140 us -> 137 us (0.979)
  starting transfers between devices: 23.1 us -> 21.3 us
  blocking collectives: 71 us -> 69.2 us
    all_to_all x2 -> x1, blocking collectives: 20.3 us -> 16.8 us  [on_device(): lax.all_to_all(jnp.broadcast_to(v, (ny * nzh, *v.shape)), ('yh', 'zh'), 0...]
    ppermute x1, starting transfers between devices: 9.05 us -> 7.31 us  [on_device(): other = lax.ppermute(v, 'core', swap)]
    all_to_all x1, blocking collectives: 15.4 us -> 17.2 us  [on_device(): lax.all_to_all(jnp.broadcast_to(v, (nb, *v.shape)), block, 0, 0, tiled=True)]
where the time goes in v5:
time: 137 us
  blocking collectives  69.2 us (51%)
  Pallas kernels  38.9 us (28%)
  starting transfers between devices  21.3 us (16%)
  waiting for transfers between devices  4.61 us (3%)
    pallas_call x5, Pallas kernels, call(): pl.pallas_call(kernel, out_shape=outs, in_specs=([SMEM] if where is not N...  38.9 us
    all_to_all x1, blocking collectives, on_device(): lax.all_to_all(v.reshape(nb, half // nb, NB), block, 0, 0, tiled=True)  22.5 us
    all_to_all x1, blocking collectives, on_device(): lax.all_to_all(jnp.broadcast_to(v, (nb, *v.shape)), block, 0, 0, tiled=True)  17.2 us
    all_to_all x1, blocking collectives, on_device(): lax.all_to_all(jnp.broadcast_to(v, (ny * nzh, *v.shape)), ('yh', 'zh'), 0...  16.8 us
    all_to_all x1, blocking collectives, on_device(): lax.all_to_all(v.reshape(ny, 1, v.size // ny), 'yh', 0, 0, tiled=True)  12.7 us
    all_to_all x1, starting transfers between devices, on_device(): owned = lax.all_to_all(partial, ('zh', 'zl', 'core'), 0, 0, tiled=True)  11.8 us
    ppermute x1, starting transfers between devices, on_device(): other = lax.ppermute(v, 'core', swap)  7.31 us
  transfers between devices with their start and end apart: 3, of which 2 were waited for; matrix products, arithmetic and copies ran while one was open for 0% of the time, Pallas kernels for 5%

profile of v5, /device:TPU:1, one launch (start us, length us, event | category | flops | bytes accessed | tf_op | source)
XLA Modules:
  0.0 137.1 jit_solution(8586350029488649192)
XLA Ops:
  0.7 3.2 %arcs.1 = (f32[16,4,1152]{2,1,0:T(4,128)}, f32[8,128]{1,0:T(8,128)}) custom-call(f32[512,1024]{1,0:T(8,128)} %design_ref.1, f32[1,512]{1,0:T(1,128)} %bitcast.14, f32[1,512]{1,0:T(1,128)} %bitcast.16, s32[1,512]{1,0:T(1,128)} %bitcast.20), custom_call_target="tpu_custom_call" | custom-call | tf_op jit(solution)/shard_map/arcs/pallas_call | solution.py:341
  3.9 11.8 %all-to-all-start = ((f32[16,4,1152]{2,1,0:T(4,128)}), f32[16,4,1152]{2,1,0:T(4,128)}, u32[]{:S(2)}, u32[]{:S(2)}) async-start(f32[16,4,1152]{2,1,0:T(4,128)} %get-tuple-element.15), calls=%async_computation | async-start | bytes 589824 | tf_op jit(solution)/shard_map/all_to_all | solution.py:388
  15.8 0.1 pad_add_fusion.1.where_ref
  15.9 0.7 copy-done.4
  16.6 4.8 %first.1 = (f32[2304,128]{1,0:T(8,128)}, bf16[1024,1280]{1,0:T(8,128)(2,1)S(1)}, bf16[1280,1024]{1,0:T(8,128)(2,1)S(1)}, f32[8,1024]{1,0:T(8,128)S(1)}) custom-call(s32[2]{0:T(128)S(1)} %pad_add_fusion.1.where_ref, f32[512,1024]{1,0:T(8,128)S(1)} %copy-done, f32[1,512]{1,0:T(1,128)S(1)} %bitcast.15, f32[1,512]{1,0:T(1,128)S(1)} %bitcast.17, ...), custom_call_target="tpu_custom_call" | custom-call | flops 199999995904 | bytes 10000000 | tf_op jit(solution)/shard_map/first/pallas_call | solution.py:341
  21.4 2.2 %collective-permute-start = (f32[2304,128]{1,0:T(8,128)}, f32[2304,128]{1,0:T(8,128)}, u32[]{:S(2)}, u32[]{:S(2)}) collective-permute-start(f32[2304,128]{1,0:T(8,128)} %get-tuple-element.14), channel_id=1, source_target_pairs={{0,1},{1,0},{2,3},{3,2},{4,5},{5,4},{6,7},{7,6},{8,9},{9,8},{10,11... | collective-permute-start | bytes 3538952 | tf_op jit(solution)/shard_map/ppermute | solution.py:409
  23.6 2.2 %keep.1.mine_ref = f32[2304,128]{1,0:T(8,128)S(1)} custom-call(s32[2]{0:T(128)S(1)} %pad_add_fusion.1.where_ref, bf16[1024,1280]{1,0:T(8,128)(2,1)S(1)} %get-tuple-element.11.tall_ref, bf16[1280,1024]{1,0:T(8,128)(2,1)S(1)} %get-tuple-element.12.flat_ref, f32[8,1024]{1,0:T(8,128)S(1)} %get-tuple-element.13.p_ref), custom_call_target="tpu_custom_call" | custom-call | flops 199999995904 | bytes 10000000 | tf_op jit(solution)/shard_map/keep/pallas_call | solution.py:341
  25.8 0.1 pad_add_fusion.where_ref
  25.9 2.3 %all-to-all-done.arcs_ref = f32[16,4,1152]{2,1,0:T(4,128)} async-done(((f32[16,4,1152]{2,1,0:T(4,128)}), f32[16,4,1152]{2,1,0:T(4,128)}, u32[]{:S(2)}, u32[]{:S(2)}) %all-to-all-start) | async-done | bytes 294944 | tf_op jit(solution)/shard_map/all_to_all | solution.py:388
  28.3 1.8 %pair.1 = f32[2304,128]{1,0:T(8,128)S(1)} custom-call(s32[2]{0:T(128)S(1)} %pad_add_fusion.where_ref, f32[2304,128]{1,0:T(8,128)S(1)} %keep.1.mine_ref, f32[2304,128]{1,0:T(8,128)} %collective-permute-done.got_ref, f32[16,4,1152]{2,1,0:T(4,128)} %all-to-all-done.arcs_ref), custom_call_target="tpu_custom_call" | custom-call | tf_op jit(solution)/shard_map/pair/pallas_call | solution.py:341
  30.1 22.5 %all_to_all.25 = f32[16,144,128]{2,1,0:T(8,128)S(1)} all-to-all(f32[16,144,128]{2,1,0:T(8,128)S(1)} %bitcast.13), channel_id=1, replica_groups=mesh['x'=4,'yh'=4,'yl'=2,'zh'=4,'zl'=2,'core'=2] {'x','yl','zl'}, dimensions={0} | all-to-all | bytes 2359296 | tf_op jit(solution)/shard_map/all_to_all | solution.py:416
  52.6 0.1 reduce_sum.27
  52.7 12.7 %all_to_all.26 = f32[4,1,4608]{2,1,0:T(1,128)S(1)} all-to-all(f32[4,1,4608]{2,1,0:T(1,128)S(1)} %bitcast.19), channel_id=1, replica_groups=mesh['x'=4,'yh'=4,'yl'=2,'zh'=4,'zl'=2,'core'=2] {'yh'}, dimensions={0} | all-to-all | bytes 147456 | tf_op jit(solution)/shard_map/all_to_all | solution.py:417
  65.3 0.1 reduce_sum.28
  65.4 0.2 broadcast_in_dim.6
  65.6 16.8 %all_to_all.27 = f32[16,1,4608]{2,1,0:T(1,128)S(1)} all-to-all(f32[16,1,4608]{2,1,0:T(1,128)S(1)} %broadcast_in_dim.6), channel_id=1, replica_groups=mesh['x'=4,'yh'=4,'yl'=2,'zh'=4,'zl'=2,'core'=2] {'yh','zh'}, dimensions={0} | all-to-all | bytes 589824 | tf_op jit(solution)/shard_map/all_to_all | solution.py:418
  82.4 0.7 reduce.2
  83.1 0.1 reshape.45
  83.2 0.2 reduce_sum.29
  83.5 0.1 broadcast_in_dim.7
  83.5 17.2 %all_to_all.28 = f32[16,144,128]{2,1,0:T(8,128)S(1)} all-to-all(f32[16,144,128]{2,1,0:T(8,128)S(1)} %broadcast_in_dim.7), channel_id=1, replica_groups=mesh['x'=4,'yh'=4,'yl'=2,'zh'=4,'zl'=2,'core'=2] {'x','yl','zl'}, dimensions={0} | all-to-all | bytes 2359296 | tf_op jit(solution)/shard_map/all_to_all | solution.py:420
  100.7 7.3 %collective-permute-start.1 = (f32[2304,128]{1,0:T(8,128)S(1)}, f32[2304,128]{1,0:T(8,128)S(1)}, u32[]{:S(2)}, u32[]{:S(2)}) collective-permute-start(f32[2304,128]{1,0:T(8,128)S(1)} %bitcast.11), channel_id=1, source_target_pairs={{0,1},{1,0},{2,3},{3,2},{4,5},{5,4},{6,7},{7,6},{8,9},{9,8},{10,11... | collective-permute-start | bytes 3538952 | tf_op jit(solution)/shard_map/ppermute | solution.py:422
  108.0 2.3 %collective-permute-done.1.other_ref = f32[2304,128]{1,0:T(8,128)S(1)} collective-permute-done((f32[2304,128]{1,0:T(8,128)S(1)}, f32[2304,128]{1,0:T(8,128)S(1)}, u32[]{:S(2)}, u32[]{:S(2)}) %collective-permute-start.1) | collective-permute-done | bytes 1179680 | tf_op jit(solution)/shard_map/ppermute | solution.py:422
  110.3 26.8 %factor.1 = (f32[64,1024]{1,0:T(8,128)}, f32[1,64]{1,0:T(1,128)}) custom-call(s32[2]{0:T(128)S(1)} %pad_add_fusion.where_ref, f32[2304,128]{1,0:T(8,128)S(1)} %bitcast.12, f32[2304,128]{1,0:T(8,128)S(1)} %collective-permute-done.1.other_ref), custom_call_target="tpu_custom_call" | custom-call | tf_op jit(solution)/shard_map/factor/pallas_call | solution.py:341
  (13 shorter events, 0.1 us)
Async XLA Ops:
  0.6 15.2 %copy-start = (f32[512,1024]{1,0:T(8,128)S(1)}, f32[512,1024]{1,0:T(8,128)}, u32[]{:S(2)}) copy-start(f32[512,1024]{1,0:T(8,128)} %design_ref.1) | copy-start | bytes 6291460
  0.6 15.2 %copy-start.1 = (f32[512]{0:T(512)S(1)}, f32[512]{0:T(512)}, u32[]{:S(2)}) copy-start(f32[512]{0:T(512)} %param.8) | copy-start | bytes 6148
  0.7 15.2 %copy-start.2 = (f32[512]{0:T(512)S(1)}, f32[512]{0:T(512)}, u32[]{:S(2)}) copy-start(f32[512]{0:T(512)} %param.7) | copy-start | bytes 6148
  0.7 15.2 %copy-start.3 = (f32[64,1024]{1,0:T(8,128)S(1)}, f32[64,1024]{1,0:T(8,128)}, u32[]{:S(2)}) copy-start(f32[64,1024]{1,0:T(8,128)} %prior_ref.1) | copy-start | bytes 786436
  0.7 15.2 %copy-start.5 = (f32[64]{0:T(128)S(1)}, f32[64]{0:T(128)}, u32[]{:S(2)}) copy-start(f32[64]{0:T(128)} %param.11) | copy-start | bytes 772
  3.9 24.3 %all-to-all-start = ((f32[16,4,1152]{2,1,0:T(4,128)}), f32[16,4,1152]{2,1,0:T(4,128)}, u32[]{:S(2)}, u32[]{:S(2)}) async-start(f32[16,4,1152]{2,1,0:T(4,128)} %get-tuple-element.15), calls=%async_computation | async-start | bytes 589824 | tf_op jit(solution)/shard_map/all_to_all | solution.py:388
  15.9 0.7 copy-start.4
  21.4 6.8 %collective-permute-start = (f32[2304,128]{1,0:T(8,128)}, f32[2304,128]{1,0:T(8,128)}, u32[]{:S(2)}, u32[]{:S(2)}) collective-permute-start(f32[2304,128]{1,0:T(8,128)} %get-tuple-element.14), channel_id=1, source_target_pairs={{0,1},{1,0},{2,3},{3,2},{4,5},{5,4},{6,7},{7,6},{8,9},{9,8},{10,11... | collective-permute-start | bytes 3538952 | tf_op jit(solution)/shard_map/ppermute | solution.py:409
  100.7 9.6 %collective-permute-start.1 = (f32[2304,128]{1,0:T(8,128)S(1)}, f32[2304,128]{1,0:T(8,128)S(1)}, u32[]{:S(2)}, u32[]{:S(2)}) collective-permute-start(f32[2304,128]{1,0:T(8,128)S(1)} %bitcast.11), channel_id=1, source_target_pairs={{0,1},{1,0},{2,3},{3,2},{4,5},{5,4},{6,7},{7,6},{8,9},{9,8},{10,11... | collective-permute-start | bytes 3538952 | tf_op jit(solution)/shard_map/ppermute | solution.py:422

commit v6 on v5

--- a/solution.py
+++ b/solution.py
@@ -181,7 +181,7 @@
     return [pl.ds(r, NB) for r in range(0, rows, NB)]
 
 
-def arcs_kernel(design_hbm, weight_hbm, obs_hbm, arc_hbm, out_ref, done_ref, design_ref, weight_ref, obs_ref, arc_ref, sem):
+def arcs_kernel(design_hbm, weight_hbm, obs_hbm, arc_hbm, out_ref, p_ref, design_ref, weight_ref, obs_ref, arc_ref, sem):
     rows, width = design_ref.shape
     pieces, each = out_ref.shape[:2]
     arcs = pieces * each // 2
@@ -193,7 +193,6 @@
     )
     for copy in copies[:3]:
         copy.wait()
-    done_ref[...] = jnp.zeros_like(done_ref)
     w = weight_ref[...]
     number = lax.broadcasted_iota(jnp.int32, (arcs, rows), 0)
     member = jnp.where(number == arc_ref[...], w * w, 0.0)
@@ -201,12 +200,14 @@
     obs = jnp.sum(member * obs_ref[...], axis=1, keepdims=True)
     lane = lax.broadcasted_iota(jnp.int32, (arcs, NB), 1)
     tail = jnp.where(lane == 0, obs, jnp.where(lane == 1, total, 0.0))
+    ask = jnp.concatenate([member, jnp.broadcast_to(w * w * obs_ref[...], (8, rows))], axis=0)
     sums = None
     for n, p in enumerate(parts):
         copies[3 + n].wait()
-        more = exact(member[:, n * NB:(n + 1) * NB], design_ref[p, :])
+        more = exact(ask[:, n * NB:(n + 1) * NB], design_ref[p, :])
         sums = more if sums is None else sums + more
-    sums = jnp.concatenate([sums, tail], axis=1)
+    p_ref[...] = sums[arcs:]
+    sums = jnp.concatenate([sums[:arcs], tail], axis=1)
     for n in range(pieces):
         at = n // 2 * each
         out_ref[n] = sums[at:at + each]
@@ -248,14 +249,13 @@
 
 
 def first_kernel(
-    where_ref, design_ref, weight_ref, obs_ref, prior_ref, prhs_ref, after_ref, out_ref, tall_ref, flat_ref, p_ref
+    where_ref, design_ref, weight_ref, prior_ref, prhs_ref, data_ref, out_ref, tall_ref, flat_ref, p_ref
 ):
     rows, width = design_ref.shape
     prows = prior_ref.shape[0]
     deep = tall_ref.shape[1] // 2
     include = where_ref[1].astype(f32)
     w = weight_ref[...]
-    wobs = jnp.broadcast_to(w * w * obs_ref[...], (8, rows))
 
     def place(r, z):
         for c in range(0, width, NB):
@@ -273,7 +273,7 @@
         place(r, design_ref[r:r + NB, :] * jnp.concatenate([column] * (width // NB), axis=1))
     prior = prior_ref[...] * include
     place(rows, jnp.concatenate([prior, jnp.zeros((NB - prows, width), f32)], axis=0))
-    p_ref[...] = exact(wobs, design_ref[...]) + exact(jnp.broadcast_to(prhs_ref[...], (8, prows)), prior)
+    p_ref[...] = data_ref[...] + exact(jnp.broadcast_to(prhs_ref[...], (8, prows)), prior)
     half_kernel(False, where_ref, tall_ref, flat_ref, p_ref, out_ref)
 
 
@@ -369,12 +369,12 @@
     nparts = rows // NB
     deep = rows + NB
     here = jnp.stack([core, include]).astype(jnp.int32)
-    partial, done = call(
+    partial, p_data = call(
         arcs_kernel,
         "arcs",
         None,
         (design, weight, obs, arc),
-        (like(nz * nc, 2 * nc, width + NB), like(8, NB)),
+        (like(nz * nc, 2 * nc, width + NB), like(8, width)),
         [
             pltpu.VMEM((rows, width), f32),
             pltpu.VMEM((1, rows), f32),
@@ -391,32 +391,33 @@
         first_kernel,
         "first",
         here,
-        (design, weight, obs, prior_factor, prior_rhs.reshape(1, prows), done),
+        (design, weight, prior_factor, prior_rhs.reshape(1, prows), p_data),
         (
-            like(half, NB),
+            pltpu.VMEM((half, NB), f32),
             pltpu.VMEM((width, 2 * deep), bf16),
             pltpu.VMEM((2 * deep, width), bf16),
             pltpu.VMEM((8, width), f32),
         ),
         [],
-        20,
+        14,
         cost=work,
     )
     keep = call(
-        functools.partial(half_kernel, True), "keep", here, (tall, flat, p), pltpu.VMEM((half, NB), f32), [], 20, cost=work
+        functools.partial(half_kernel, True), "keep", here, (tall, flat, p), pltpu.VMEM((half, NB), f32), [], 10, cost=work
     )
     swap = [(i, 1 - i) for i in range(nc)]
     got = lax.ppermute(send, "core", swap)
     where = jnp.stack([core, z * nc + core]).astype(jnp.int32)
     v = call(
-        pair_kernel, "pair", where, (keep, got, owned), like(half, NB), [], 32
+        pair_kernel, "pair", where, (keep, got, owned), like(half, NB), [], 10
     )
     block = ("x", "yl", "zl")
     nb, ny, nzh = (lax.axis_size(a) for a in (block, "yh", "zh"))
     v = lax.all_to_all(v.reshape(nb, half // nb, NB), block, 0, 0, tiled=True).sum(0)
     v = lax.all_to_all(v.reshape(ny, 1, v.size // ny), "yh", 0, 0, tiled=True).sum(0)
     v = lax.all_to_all(jnp.broadcast_to(v, (ny * nzh, *v.shape)), ("yh", "zh"), 0, 0, tiled=True)
-    v = v.reshape(ny, nzh, 1, v.shape[-1]).sum(1).reshape(half // nb, NB)
+    v = v.reshape(ny, nzh, 1, v.shape[-1])
+    v = functools.reduce(jnp.add, [v[:, n] for n in range(nzh)]).reshape(half // nb, NB)
     v = lax.all_to_all(jnp.broadcast_to(v, (nb, *v.shape)), block, 0, 0, tiled=True)
     v = v.reshape(half, NB)
     other = lax.ppermute(v, "core", swap)

time: 137 us -> 136 us (level)
  no operation moved by 1% of the time
where the time goes in v6:
time: 136 us
  blocking collectives  68.7 us (51%)
  Pallas kernels  38.3 us (28%)
  starting transfers between devices  21.3 us (16%)
  waiting for transfers between devices  5.11 us (4%)
    pallas_call x5, Pallas kernels, call(): pl.pallas_call(kernel, out_shape=outs, in_specs=([SMEM] if where is not N...  38.3 us
    all_to_all x1, blocking collectives, on_device(): lax.all_to_all(v.reshape(nb, half // nb, NB), block, 0, 0, tiled=True)  22.8 us
    all_to_all x1, blocking collectives, on_device(): lax.all_to_all(jnp.broadcast_to(v, (nb, *v.shape)), block, 0, 0, tiled=True)  17.2 us
    all_to_all x1, blocking collectives, on_device(): lax.all_to_all(jnp.broadcast_to(v, (ny * nzh, *v.shape)), ('yh', 'zh'), 0...  16 us
    all_to_all x1, blocking collectives, on_device(): lax.all_to_all(v.reshape(ny, 1, v.size // ny), 'yh', 0, 0, tiled=True)  12.7 us
    all_to_all x1, starting transfers between devices, on_device(): owned = lax.all_to_all(partial, ('zh', 'zl', 'core'), 0, 0, tiled=True)  11.8 us
    ppermute x1, starting transfers between devices, on_device(): other = lax.ppermute(v, 'core', swap)  7.31 us
    all_to_all x1, waiting for transfers between devices, on_device(): owned = lax.all_to_all(partial, ('zh', 'zl', 'core'), 0, 0, tiled=True)  2.84 us
  transfers between devices with their start and end apart: 3, of which 2 were waited for; matrix products, arithmetic and copies ran while one was open for 0% of the time, Pallas kernels for 5%

profile of v6, /device:TPU:1, one launch (start us, length us, event | category | flops | bytes accessed | tf_op | source)
XLA Modules:
  0.0 135.6 jit_solution(3935753902422857518)
XLA Ops:
  0.7 3.2 %arcs.1 = (f32[16,4,1152]{2,1,0:T(4,128)}, f32[8,1024]{1,0:T(8,128)}) custom-call(f32[512,1024]{1,0:T(8,128)} %design_ref.1, f32[1,512]{1,0:T(1,128)} %bitcast.16, f32[1,512]{1,0:T(1,128)} %bitcast.22, s32[1,512]{1,0:T(1,128)} %bitcast.23), custom_call_target="tpu_custom_call" | custom-call | tf_op jit(solution)/shard_map/arcs/pallas_call | solution.py:341
  3.9 11.8 %all-to-all-start = ((f32[16,4,1152]{2,1,0:T(4,128)}), f32[16,4,1152]{2,1,0:T(4,128)}, u32[]{:S(2)}, u32[]{:S(2)}) async-start(f32[16,4,1152]{2,1,0:T(4,128)} %get-tuple-element.15), calls=%async_computation | async-start | bytes 589824 | tf_op jit(solution)/shard_map/all_to_all | solution.py:388
  15.8 0.1 pad_add_fusion.1.where_ref
  15.9 0.0 copy-start.3
  15.9 0.7 copy-done.3
  16.6 4.3 %first.1 = (f32[2304,128]{1,0:T(8,128)}, bf16[1024,1280]{1,0:T(8,128)(2,1)S(1)}, bf16[1280,1024]{1,0:T(8,128)(2,1)S(1)}, f32[8,1024]{1,0:T(8,128)S(1)}) custom-call(s32[2]{0:T(128)S(1)} %pad_add_fusion.1.where_ref, f32[512,1024]{1,0:T(8,128)S(1)} %copy-done, f32[1,512]{1,0:T(1,128)S(1)} %bitcast.17, f32[64,1024]{1,0:T(8,128)S(1)} %copy-done.2, ...), custom_call_target="tpu_custom_call" | custom-call | flops 199999995904 | bytes 10000000 | tf_op jit(solution)/shard_map/first/pallas_call | solution.py:341
  20.9 2.2 %collective-permute-start = (f32[2304,128]{1,0:T(8,128)}, f32[2304,128]{1,0:T(8,128)}, u32[]{:S(2)}, u32[]{:S(2)}) collective-permute-start(f32[2304,128]{1,0:T(8,128)} %get-tuple-element.14), channel_id=1, source_target_pairs={{0,1},{1,0},{2,3},{3,2},{4,5},{5,4},{6,7},{7,6},{8,9},{9,8},{10,11... | collective-permute-start | bytes 3538952 | tf_op jit(solution)/shard_map/ppermute | solution.py:409
  23.1 2.2 %keep.1.mine_ref = f32[2304,128]{1,0:T(8,128)S(1)} custom-call(s32[2]{0:T(128)S(1)} %pad_add_fusion.1.where_ref, bf16[1024,1280]{1,0:T(8,128)(2,1)S(1)} %get-tuple-element.11.tall_ref, bf16[1280,1024]{1,0:T(8,128)(2,1)S(1)} %get-tuple-element.12.flat_ref, f32[8,1024]{1,0:T(8,128)S(1)} %get-tuple-element.13.p_ref), custom_call_target="tpu_custom_call" | custom-call | flops 199999995904 | bytes 10000000 | tf_op jit(solution)/shard_map/keep/pallas_call | solution.py:341
  25.3 0.1 pad_add_fusion.where_ref
  25.4 2.8 %all-to-all-done.arcs_ref = f32[16,4,1152]{2,1,0:T(4,128)} async-done(((f32[16,4,1152]{2,1,0:T(4,128)}), f32[16,4,1152]{2,1,0:T(4,128)}, u32[]{:S(2)}, u32[]{:S(2)}) %all-to-all-start) | async-done | bytes 294944 | tf_op jit(solution)/shard_map/all_to_all | solution.py:388
  28.2 0.0 collective-permute-done.got_ref
  28.2 1.8 %pair.1 = f32[2304,128]{1,0:T(8,128)S(1)} custom-call(s32[2]{0:T(128)S(1)} %pad_add_fusion.where_ref, f32[2304,128]{1,0:T(8,128)S(1)} %keep.1.mine_ref, f32[2304,128]{1,0:T(8,128)} %collective-permute-done.got_ref, f32[16,4,1152]{2,1,0:T(4,128)} %all-to-all-done.arcs_ref), custom_call_target="tpu_custom_call" | custom-call | tf_op jit(solution)/shard_map/pair/pallas_call | solution.py:341
  30.1 22.8 %all_to_all.25 = f32[16,144,128]{2,1,0:T(8,128)S(1)} all-to-all(f32[16,144,128]{2,1,0:T(8,128)S(1)} %bitcast.15), channel_id=1, replica_groups=mesh['x'=4,'yh'=4,'yl'=2,'zh'=4,'zl'=2,'core'=2] {'x','yl','zl'}, dimensions={0} | all-to-all | bytes 2359296 | tf_op jit(solution)/shard_map/all_to_all | solution.py:416
  52.9 0.1 reduce_sum.18
  52.9 12.7 %all_to_all.26 = f32[4,1,4608]{2,1,0:T(1,128)S(1)} all-to-all(f32[4,1,4608]{2,1,0:T(1,128)S(1)} %bitcast.20), channel_id=1, replica_groups=mesh['x'=4,'yh'=4,'yl'=2,'zh'=4,'zl'=2,'core'=2] {'yh'}, dimensions={0} | all-to-all | bytes 147456 | tf_op jit(solution)/shard_map/all_to_all | solution.py:417
  65.7 0.1 reduce_sum.19
  65.8 0.2 broadcast_in_dim.6
  65.9 16.0 %all_to_all.27 = f32[16,1,4608]{2,1,0:T(1,128)S(1)} all-to-all(f32[16,1,4608]{2,1,0:T(1,128)S(1)} %broadcast_in_dim.6), channel_id=1, replica_groups=mesh['x'=4,'yh'=4,'yl'=2,'zh'=4,'zl'=2,'core'=2] {'yh','zh'}, dimensions={0} | all-to-all | bytes 589824 | tf_op jit(solution)/shard_map/all_to_all | solution.py:418
  81.9 0.1 slice_add_fusion
  82.0 0.1 broadcast_in_dim.7
  82.1 17.2 %all_to_all.28 = f32[16,144,128]{2,1,0:T(8,128)S(1)} all-to-all(f32[16,144,128]{2,1,0:T(8,128)S(1)} %broadcast_in_dim.7), channel_id=1, replica_groups=mesh['x'=4,'yh'=4,'yl'=2,'zh'=4,'zl'=2,'core'=2] {'x','yl','zl'}, dimensions={0} | all-to-all | bytes 2359296 | tf_op jit(solution)/shard_map/all_to_all | solution.py:421
  99.3 7.3 %collective-permute-start.1 = (f32[2304,128]{1,0:T(8,128)S(1)}, f32[2304,128]{1,0:T(8,128)S(1)}, u32[]{:S(2)}, u32[]{:S(2)}) collective-permute-start(f32[2304,128]{1,0:T(8,128)S(1)} %bitcast.13), channel_id=1, source_target_pairs={{0,1},{1,0},{2,3},{3,2},{4,5},{5,4},{6,7},{7,6},{8,9},{9,8},{10,11... | collective-permute-start | bytes 3538952 | tf_op jit(solution)/shard_map/ppermute | solution.py:423
  106.6 2.3 %collective-permute-done.1.other_ref = f32[2304,128]{1,0:T(8,128)S(1)} collective-permute-done((f32[2304,128]{1,0:T(8,128)S(1)}, f32[2304,128]{1,0:T(8,128)S(1)}, u32[]{:S(2)}, u32[]{:S(2)}) %collective-permute-start.1) | collective-permute-done | bytes 1179680 | tf_op jit(solution)/shard_map/ppermute | solution.py:423
  108.9 26.8 %factor.1 = (f32[64,1024]{1,0:T(8,128)}, f32[1,64]{1,0:T(1,128)}) custom-call(s32[2]{0:T(128)S(1)} %pad_add_fusion.where_ref, f32[2304,128]{1,0:T(8,128)S(1)} %bitcast.14, f32[2304,128]{1,0:T(8,128)S(1)} %collective-permute-done.1.other_ref), custom_call_target="tpu_custom_call" | custom-call | tf_op jit(solution)/shard_map/factor/pallas_call | solution.py:341
  (8 shorter events, 0.0 us)
Async XLA Ops:
  0.6 15.2 %copy-start = (f32[512,1024]{1,0:T(8,128)S(1)}, f32[512,1024]{1,0:T(8,128)}, u32[]{:S(2)}) copy-start(f32[512,1024]{1,0:T(8,128)} %design_ref.1) | copy-start | bytes 6291460
  0.6 15.2 %copy-start.1 = (f32[512]{0:T(512)S(1)}, f32[512]{0:T(512)}, u32[]{:S(2)}) copy-start(f32[512]{0:T(512)} %param.8) | copy-start | bytes 6148
  0.7 15.2 %copy-start.2 = (f32[64,1024]{1,0:T(8,128)S(1)}, f32[64,1024]{1,0:T(8,128)}, u32[]{:S(2)}) copy-start(f32[64,1024]{1,0:T(8,128)} %prior_ref.1) | copy-start | bytes 786436
  0.7 15.2 %copy-start.4 = (f32[64]{0:T(128)S(1)}, f32[64]{0:T(128)}, u32[]{:S(2)}) copy-start(f32[64]{0:T(128)} %param.11) | copy-start | bytes 772
  3.9 24.3 %all-to-all-start = ((f32[16,4,1152]{2,1,0:T(4,128)}), f32[16,4,1152]{2,1,0:T(4,128)}, u32[]{:S(2)}, u32[]{:S(2)}) async-start(f32[16,4,1152]{2,1,0:T(4,128)} %get-tuple-element.15), calls=%async_computation | async-start | bytes 589824 | tf_op jit(solution)/shard_map/all_to_all | solution.py:388
  15.9 0.8 copy-start.3
  20.9 7.3 %collective-permute-start = (f32[2304,128]{1,0:T(8,128)}, f32[2304,128]{1,0:T(8,128)}, u32[]{:S(2)}, u32[]{:S(2)}) collective-permute-start(f32[2304,128]{1,0:T(8,128)} %get-tuple-element.14), channel_id=1, source_target_pairs={{0,1},{1,0},{2,3},{3,2},{4,5},{5,4},{6,7},{7,6},{8,9},{9,8},{10,11... | collective-permute-start | bytes 3538952 | tf_op jit(solution)/shard_map/ppermute | solution.py:409
  99.3 9.6 %collective-permute-start.1 = (f32[2304,128]{1,0:T(8,128)S(1)}, f32[2304,128]{1,0:T(8,128)S(1)}, u32[]{:S(2)}, u32[]{:S(2)}) collective-permute-start(f32[2304,128]{1,0:T(8,128)S(1)} %bitcast.13), channel_id=1, source_target_pairs={{0,1},{1,0},{2,3},{3,2},{4,5},{5,4},{6,7},{7,6},{8,9},{9,8},{10,11... | collective-permute-start | bytes 3538952 | tf_op jit(solution)/shard_map/ppermute | solution.py:423

commit v7 on v6

--- a/solution.py
+++ b/solution.py
@@ -68,7 +68,10 @@
                 head = spread(col[j][kh], k % 8)
                 heads[j, k] = head
                 for c in own[k // 8:]:
-                    col[k][c] = col[k][c] - scaled[c] * head
+                    if k == j + 1 and c == kh:
+                        col[k][c] = col[k][c] - (col[j][c] * head) * q
+                    else:
+                        col[k][c] = col[k][c] - scaled[c] * head
             sx, sy = spread(x[home], j % 8), spread(y[home], j % 8)
             for c in own[j // 8:]:
                 m = jnp.where(sub > j % 8, scaled[c], 0.0) if c == home else scaled[c]

time: 136 us -> 136 us (level)
  no operation moved by 1% of the time
where the time goes in v7:
time: 136 us; the launch traced here: 135 us
  blocking collectives  68.7 us (51%)
  Pallas kernels  38 us (28%)
  starting transfers between devices  21.3 us (16%)
  waiting for transfers between devices  5.11 us (4%)
    pallas_call x5, Pallas kernels, call(): pl.pallas_call(kernel, out_shape=outs, in_specs=([SMEM] if where is not N...  38 us
    all_to_all x1, blocking collectives, on_device(): lax.all_to_all(v.reshape(nb, half // nb, NB), block, 0, 0, tiled=True)  22.8 us
    all_to_all x1, blocking collectives, on_device(): lax.all_to_all(jnp.broadcast_to(v, (nb, *v.shape)), block, 0, 0, tiled=True)  17.2 us
    all_to_all x1, blocking collectives, on_device(): lax.all_to_all(jnp.broadcast_to(v, (ny * nzh, *v.shape)), ('yh', 'zh'), 0...  16 us
    all_to_all x1, blocking collectives, on_device(): lax.all_to_all(v.reshape(ny, 1, v.size // ny), 'yh', 0, 0, tiled=True)  12.7 us
    all_to_all x1, starting transfers between devices, on_device(): owned = lax.all_to_all(partial, ('zh', 'zl', 'core'), 0, 0, tiled=True)  11.8 us
    ppermute x1, starting transfers between devices, on_device(): other = lax.ppermute(v, 'core', swap)  7.31 us
    all_to_all x1, waiting for transfers between devices, on_device(): owned = lax.all_to_all(partial, ('zh', 'zl', 'core'), 0, 0, tiled=True)  2.84 us
  transfers between devices with their start and end apart: 3, of which 2 were waited for; matrix products, arithmetic and copies ran while one was open for 0% of the time, Pallas kernels for 5%

profile of v7, /device:TPU:1, one launch (start us, length us, event | category | flops | bytes accessed | tf_op | source)
XLA Modules:
  0.0 135.3 jit_solution(6966745769870557447)
XLA Ops:
  0.7 3.2 %arcs.1 = (f32[16,4,1152]{2,1,0:T(4,128)}, f32[8,1024]{1,0:T(8,128)}) custom-call(f32[512,1024]{1,0:T(8,128)} %design_ref.1, f32[1,512]{1,0:T(1,128)} %bitcast.16, f32[1,512]{1,0:T(1,128)} %bitcast.22, s32[1,512]{1,0:T(1,128)} %bitcast.23), custom_call_target="tpu_custom_call" | custom-call | tf_op jit(solution)/shard_map/arcs/pallas_call | solution.py:344
  3.9 11.8 %all-to-all-start = ((f32[16,4,1152]{2,1,0:T(4,128)}), f32[16,4,1152]{2,1,0:T(4,128)}, u32[]{:S(2)}, u32[]{:S(2)}) async-start(f32[16,4,1152]{2,1,0:T(4,128)} %get-tuple-element.15), calls=%async_computation | async-start | bytes 589824 | tf_op jit(solution)/shard_map/all_to_all | solution.py:391
  15.8 0.1 pad_add_fusion.1.where_ref
  15.9 0.0 copy-start.3
  15.9 0.7 copy-done.3
  16.6 4.3 %first.1 = (f32[2304,128]{1,0:T(8,128)}, bf16[1024,1280]{1,0:T(8,128)(2,1)S(1)}, bf16[1280,1024]{1,0:T(8,128)(2,1)S(1)}, f32[8,1024]{1,0:T(8,128)S(1)}) custom-call(s32[2]{0:T(128)S(1)} %pad_add_fusion.1.where_ref, f32[512,1024]{1,0:T(8,128)S(1)} %copy-done, f32[1,512]{1,0:T(1,128)S(1)} %bitcast.17, f32[64,1024]{1,0:T(8,128)S(1)} %copy-done.2, ...), custom_call_target="tpu_custom_call" | custom-call | flops 199999995904 | bytes 10000000 | tf_op jit(solution)/shard_map/first/pallas_call | solution.py:344
  20.9 2.2 %collective-permute-start = (f32[2304,128]{1,0:T(8,128)}, f32[2304,128]{1,0:T(8,128)}, u32[]{:S(2)}, u32[]{:S(2)}) collective-permute-start(f32[2304,128]{1,0:T(8,128)} %get-tuple-element.14), channel_id=1, source_target_pairs={{0,1},{1,0},{2,3},{3,2},{4,5},{5,4},{6,7},{7,6},{8,9},{9,8},{10,11... | collective-permute-start | bytes 3538952 | tf_op jit(solution)/shard_map/ppermute | solution.py:412
  23.1 2.2 %keep.1.mine_ref = f32[2304,128]{1,0:T(8,128)S(1)} custom-call(s32[2]{0:T(128)S(1)} %pad_add_fusion.1.where_ref, bf16[1024,1280]{1,0:T(8,128)(2,1)S(1)} %get-tuple-element.11.tall_ref, bf16[1280,1024]{1,0:T(8,128)(2,1)S(1)} %get-tuple-element.12.flat_ref, f32[8,1024]{1,0:T(8,128)S(1)} %get-tuple-element.13.p_ref), custom_call_target="tpu_custom_call" | custom-call | flops 199999995904 | bytes 10000000 | tf_op jit(solution)/shard_map/keep/pallas_call | solution.py:344
  25.3 0.1 pad_add_fusion.where_ref
  25.4 2.8 %all-to-all-done.arcs_ref = f32[16,4,1152]{2,1,0:T(4,128)} async-done(((f32[16,4,1152]{2,1,0:T(4,128)}), f32[16,4,1152]{2,1,0:T(4,128)}, u32[]{:S(2)}, u32[]{:S(2)}) %all-to-all-start) | async-done | bytes 294944 | tf_op jit(solution)/shard_map/all_to_all | solution.py:391
  28.2 0.0 collective-permute-done.got_ref
  28.2 1.8 %pair.1 = f32[2304,128]{1,0:T(8,128)S(1)} custom-call(s32[2]{0:T(128)S(1)} %pad_add_fusion.where_ref, f32[2304,128]{1,0:T(8,128)S(1)} %keep.1.mine_ref, f32[2304,128]{1,0:T(8,128)} %collective-permute-done.got_ref, f32[16,4,1152]{2,1,0:T(4,128)} %all-to-all-done.arcs_ref), custom_call_target="tpu_custom_call" | custom-call | tf_op jit(solution)/shard_map/pair/pallas_call | solution.py:344
  30.1 22.8 %all_to_all.25 = f32[16,144,128]{2,1,0:T(8,128)S(1)} all-to-all(f32[16,144,128]{2,1,0:T(8,128)S(1)} %bitcast.15), channel_id=1, replica_groups=mesh['x'=4,'yh'=4,'yl'=2,'zh'=4,'zl'=2,'core'=2] {'x','yl','zl'}, dimensions={0} | all-to-all | bytes 2359296 | tf_op jit(solution)/shard_map/all_to_all | solution.py:419
  52.9 0.1 reduce_sum.18
  52.9 12.7 %all_to_all.26 = f32[4,1,4608]{2,1,0:T(1,128)S(1)} all-to-all(f32[4,1,4608]{2,1,0:T(1,128)S(1)} %bitcast.20), channel_id=1, replica_groups=mesh['x'=4,'yh'=4,'yl'=2,'zh'=4,'zl'=2,'core'=2] {'yh'}, dimensions={0} | all-to-all | bytes 147456 | tf_op jit(solution)/shard_map/all_to_all | solution.py:420
  65.7 0.1 reduce_sum.19
  65.8 0.2 broadcast_in_dim.6
  65.9 16.0 %all_to_all.27 = f32[16,1,4608]{2,1,0:T(1,128)S(1)} all-to-all(f32[16,1,4608]{2,1,0:T(1,128)S(1)} %broadcast_in_dim.6), channel_id=1, replica_groups=mesh['x'=4,'yh'=4,'yl'=2,'zh'=4,'zl'=2,'core'=2] {'yh','zh'}, dimensions={0} | all-to-all | bytes 589824 | tf_op jit(solution)/shard_map/all_to_all | solution.py:421
  81.9 0.1 slice_add_fusion
  82.0 0.1 broadcast_in_dim.7
  82.1 17.2 %all_to_all.28 = f32[16,144,128]{2,1,0:T(8,128)S(1)} all-to-all(f32[16,144,128]{2,1,0:T(8,128)S(1)} %broadcast_in_dim.7), channel_id=1, replica_groups=mesh['x'=4,'yh'=4,'yl'=2,'zh'=4,'zl'=2,'core'=2] {'x','yl','zl'}, dimensions={0} | all-to-all | bytes 2359296 | tf_op jit(solution)/shard_map/all_to_all | solution.py:424
  99.3 7.3 %collective-permute-start.1 = (f32[2304,128]{1,0:T(8,128)S(1)}, f32[2304,128]{1,0:T(8,128)S(1)}, u32[]{:S(2)}, u32[]{:S(2)}) collective-permute-start(f32[2304,128]{1,0:T(8,128)S(1)} %bitcast.13), channel_id=1, source_target_pairs={{0,1},{1,0},{2,3},{3,2},{4,5},{5,4},{6,7},{7,6},{8,9},{9,8},{10,11... | collective-permute-start | bytes 3538952 | tf_op jit(solution)/shard_map/ppermute | solution.py:426
  106.6 2.3 %collective-permute-done.1.other_ref = f32[2304,128]{1,0:T(8,128)S(1)} collective-permute-done((f32[2304,128]{1,0:T(8,128)S(1)}, f32[2304,128]{1,0:T(8,128)S(1)}, u32[]{:S(2)}, u32[]{:S(2)}) %collective-permute-start.1) | collective-permute-done | bytes 1179680 | tf_op jit(solution)/shard_map/ppermute | solution.py:426
  108.9 26.4 %factor.1 = (f32[64,1024]{1,0:T(8,128)}, f32[1,64]{1,0:T(1,128)}) custom-call(s32[2]{0:T(128)S(1)} %pad_add_fusion.where_ref, f32[2304,128]{1,0:T(8,128)S(1)} %bitcast.14, f32[2304,128]{1,0:T(8,128)S(1)} %collective-permute-done.1.other_ref), custom_call_target="tpu_custom_call" | custom-call | tf_op jit(solution)/shard_map/factor/pallas_call | solution.py:344
  (8 shorter events, 0.0 us)
Async XLA Ops:
  0.6 15.2 %copy-start = (f32[512,1024]{1,0:T(8,128)S(1)}, f32[512,1024]{1,0:T(8,128)}, u32[]{:S(2)}) copy-start(f32[512,1024]{1,0:T(8,128)} %design_ref.1) | copy-start | bytes 6291460
  0.6 15.2 %copy-start.1 = (f32[512]{0:T(512)S(1)}, f32[512]{0:T(512)}, u32[]{:S(2)}) copy-start(f32[512]{0:T(512)} %param.8) | copy-start | bytes 6148
  0.7 15.2 %copy-start.2 = (f32[64,1024]{1,0:T(8,128)S(1)}, f32[64,1024]{1,0:T(8,128)}, u32[]{:S(2)}) copy-start(f32[64,1024]{1,0:T(8,128)} %prior_ref.1) | copy-start | bytes 786436
  0.7 15.2 %copy-start.4 = (f32[64]{0:T(128)S(1)}, f32[64]{0:T(128)}, u32[]{:S(2)}) copy-start(f32[64]{0:T(128)} %param.11) | copy-start | bytes 772
  3.9 24.3 %all-to-all-start = ((f32[16,4,1152]{2,1,0:T(4,128)}), f32[16,4,1152]{2,1,0:T(4,128)}, u32[]{:S(2)}, u32[]{:S(2)}) async-start(f32[16,4,1152]{2,1,0:T(4,128)} %get-tuple-element.15), calls=%async_computation | async-start | bytes 589824 | tf_op jit(solution)/shard_map/all_to_all | solution.py:391
  15.9 0.8 copy-start.3
  20.9 7.3 %collective-permute-start = (f32[2304,128]{1,0:T(8,128)}, f32[2304,128]{1,0:T(8,128)}, u32[]{:S(2)}, u32[]{:S(2)}) collective-permute-start(f32[2304,128]{1,0:T(8,128)} %get-tuple-element.14), channel_id=1, source_target_pairs={{0,1},{1,0},{2,3},{3,2},{4,5},{5,4},{6,7},{7,6},{8,9},{9,8},{10,11... | collective-permute-start | bytes 3538952 | tf_op jit(solution)/shard_map/ppermute | solution.py:412
  99.3 9.6 %collective-permute-start.1 = (f32[2304,128]{1,0:T(8,128)S(1)}, f32[2304,128]{1,0:T(8,128)S(1)}, u32[]{:S(2)}, u32[]{:S(2)}) collective-permute-start(f32[2304,128]{1,0:T(8,128)S(1)} %bitcast.13), channel_id=1, source_target_pairs={{0,1},{1,0},{2,3},{3,2},{4,5},{5,4},{6,7},{7,6},{8,9},{9,8},{10,11... | collective-permute-start | bytes 3538952 | tf_op jit(solution)/shard_map/ppermute | solution.py:426
